TPU v7x, 512 devices: a whole 4x4x16 slice. The times are simulated.
512 devices in a mesh: row: 32 (over y, z_lo), col: 8 (over x, core), rep: 2 (over z_hi).
Axes of the slice: x: 4, y: 4, z: 16 (z_hi: 2, z_lo: 8; z = z_hi * 8 + z_lo), core: 2. Of those that a mesh axis runs over, the one named last changes fastest.
Arguments:
- coeffs: bfloat16 [512, 98304], P('row', 'col'), may hold values from -6 to 6
- alpha_coupling: bfloat16 [512, 512], replicated, may hold values from -0.25 to 0.25
- parent_string_index: int32 [32, 98304], P('rep', 'col'), may hold values from 0 to 98303
- excitation_weight: float32 [32, 98304], P('rep', 'col'), may hold values from -1 to 1
Outputs:
- sigma: bfloat16 [512, 98304], P('row', 'col')
Inputs may be any that keep to these rules, and one draw needn't show every extreme that they name: `parent_string_index`: global index of a beta string.
All inputs are finite; a program needn't handle non-finite values.
Results may differ from a plain program's by a relative error of at most 0.0012.
Values may be sent and summed in bfloat16 or wider, within the bound.
No kernel may reach another device: no remote copies, remote signals or barrier semaphores. Data moves between devices by JAX's collectives and lax.ppermute only.
A program may use at most 192 MiB of HBM per device.

v0:
```python
import jax
import jax.numpy as jnp
from jax import lax
from jax.sharding import PartitionSpec as P


def alpha_side(tile_cols, alpha_coupling):
    row_count = tile_cols.shape[0]
    own_rows = lax.dynamic_slice_in_dim(
        alpha_coupling, lax.axis_index("row") * row_count, row_count, 0
    )
    return jnp.dot(
        own_rows,
        lax.all_gather(tile_cols, "row", axis=0, tiled=True),
        preferred_element_type=jnp.float32,
    )


def per_device(coeffs, alpha_coupling, parent_string_index, excitation_weight):
    row_count = coeffs.shape[0]
    beta_count = coeffs.shape[1]
    slot_count = parent_string_index.shape[0]
    table = lax.all_gather(coeffs.T, "col", axis=0, tiled=True)
    picked = jnp.take(table, parent_string_index.reshape(-1), axis=0)
    picked = picked.reshape(slot_count, beta_count, row_count).astype(jnp.float32)
    weighted = jnp.sum(picked * excitation_weight[:, :, None], axis=0)
    partial_value = weighted.T
    beta_sum = lax.psum(partial_value, "rep")
    return (alpha_side(coeffs, alpha_coupling) + beta_sum).astype(jnp.bfloat16)


def solution(mesh):
    placed = (P("row", "col"), P(), P("rep", "col"), P("rep", "col"))
    return jax.shard_map(
        per_device, mesh=mesh, in_specs=placed, out_specs=P("row", "col"), check_vma=False
    )
```

profile of v0, /device:TPU:1, one launch (start us, length us, event | category | flops | bytes accessed | tf_op | source)
XLA Modules:
  0.0 1247.7 jit_solution(6381612462335634469)
XLA Ops:
  7.4 0.0 copy-start
  7.4 0.0 all-gather.5.cloned.1.call-start
  7.4 3.7 copy.6
  11.0 0.0 all-gather.5.cloned.1.call-update
  11.1 0.0 all-reduce.2.cloned.1.call-start
  11.1 1.9 copy.8
  13.1 0.9 compare_select_fusion
  13.9 1.4 compare_and_fusion
  15.3 0.1 broadcast_clamp_fusion
  15.4 0.0 copy-start.1
  15.4 129.4 %all-gather.5.cloned.1.call-done = bf16[98304,16]{1,0:T(8,128)(2,1)} async-done(((bf16[12288,16]{1,0:T(8,128)(2,1)}), bf16[98304,16]{1,0:T(8,128)(2,1)}) %all-gather.5.cloned.1.call-update) | async-done | bytes 3145744 | tf_op jit(solution)/shard_map/all_gather | solution.py:23
  144.9 663.3 %gather_fusion = bf16[196608,16]{1,0:T(8,128)(2,1)} fusion(bf16[98304,16]{1,0:T(8,128)(2,1)} %all-gather.5.cloned.1.call-done, s32[196608]{0:T(1024)S(1)} %broadcast_clamp_fusion), kind=kCustom, calls=%fused_computation | custom fusion | bytes 13369344 | tf_op jit(solution)/shard_map/jit(_take)/gather | solution.py:24
  808.2 0.0 copy-done.1
  808.2 62.0 %multiply_reduce_fusion = f32[12288,16]{1,0:T(8,128)} fusion(f32[16,12288]{1,0:T(8,128)S(1)} %copy-done.1, bf16[16,12288,16]{2,1,0:T(8,128)(2,1)} %bitcast.9, pred[16,12288]{1,0:T(8,128)(4,1)S(1)} %compare_and_fusion), kind=kLoop, calls=%fused_computation.1 | loop fusion | flops 12386304 | bytes 8060928 | tf_op jit(solution)/shard_map/reduce_sum | solution.py:26
  870.2 5.2 copy.7
  875.5 0.0 all-reduce.2.cloned.1.call-update
  875.5 0.0 all-gather.3.cloned.1.call-start
  875.6 0.5 all-gather.3.cloned.1.call-update
  876.1 113.0 %all-reduce.2.cloned.1.call-done = f32[16,12288]{1,0:T(8,128)} async-done(((f32[16,12288]{1,0:T(8,128)}), f32[16,12288]{1,0:T(8,128)}) %all-reduce.2.cloned.1.call-update) | async-done | bytes 786448 | tf_op jit(solution)/shard_map/psum | solution.py:28
  989.1 244.0 %all-gather.3.cloned.1.call-done = bf16[512,12288]{1,0:T(8,128)(2,1)} async-done(((bf16[16,12288]{1,0:T(8,128)(2,1)}), bf16[512,12288]{1,0:T(8,128)(2,1)}) %all-gather.3.cloned.1.call-update) | async-done | bytes 12582928 | tf_op jit(solution)/shard_map/all_gather | solution.py:14
  1233.0 0.0 copy-done
  1233.0 7.2 fusion
Async XLA Ops:
  7.4 1225.7 %copy-start = (bf16[512,512]{1,0:T(8,128)(2,1)S(1)}, bf16[512,512]{1,0:T(8,128)(2,1)}, u32[]{:S(2)}) copy-start(bf16[512,512]{1,0:T(8,128)(2,1)} %param.5) | copy-start | bytes 1572868
  7.4 137.5 %all-gather.5.cloned.1.call-start = ((), (), s32[]{:S(2)}) async-start(), calls=%async_computation.1 | async-start | bytes 28311552 | tf_op jit(solution)/shard_map/all_gather | solution.py:23
  11.1 978.0 %all-reduce.2.cloned.1.call-start = ((), (), s32[]{:S(2)}) async-start(), calls=%async_computation.2 | async-start | bytes 1572864 | tf_op jit(solution)/shard_map/psum | solution.py:28
  15.4 792.8 %copy-start.1 = (f32[16,12288]{1,0:T(8,128)S(1)}, f32[16,12288]{1,0:T(8,128)}, u32[]{:S(2)}) copy-start(f32[16,12288]{1,0:T(8,128)} %param.7) | copy-start | bytes 2359300
  875.5 357.5 %all-gather.3.cloned.1.call-start = ((), (), s32[]{:S(2)}) async-start(), calls=%async_computation | async-start | bytes 12976128 | tf_op jit(solution)/shard_map/all_gather | solution.py:14
Sparse Core Ops, SparseCore 0:
  11.2 133.6 all-gather.4
  875.6 113.3 all-reduce.1
Sparse Core Ops, SparseCore 1:
  878.3 354.7 all-gather.2
where the time goes:
time: 1250 us
  local copies, waits for them, and re-layouts  674 us (54%)
  waiting for transfers between devices  487 us (39%)
  other arithmetic  64.4 us (5%)
  between operations  14.9 us (1%)
    gather x1, local copies, waits for them, and re-layouts, per_device(): picked = jnp.take(table, parent_string_index.reshape(-1), axis=0)  663 us
    all_gather x1, waiting for transfers between devices, alpha_side(): lax.all_gather(tile_cols, 'row', axis=0, tiled=True)  244 us
    all_gather x1, waiting for transfers between devices, per_device(): table = lax.all_gather(coeffs.T, 'col', axis=0, tiled=True)  129 us
    psum x1, waiting for transfers between devices, per_device(): beta_sum = lax.psum(partial_value, 'rep')  113 us
    reduce_sum x1, other arithmetic, per_device(): weighted = jnp.sum(picked * excitation_weight[:, :, None], axis=0)  62 us
  transfers between devices with their start and end apart: 3, of which 3 were waited for; matrix products, arithmetic and copies ran while one was open for 0% of the time, Pallas kernels for 0%

commit v1 on v0

v1 whole, which is shorter than its diff:
```python
import functools

import jax
import jax.numpy as jnp
from jax import lax
from jax.experimental import pallas as pl
from jax.experimental.pallas import tpu as pltpu
from jax.sharding import PartitionSpec as P

Y = 4
Z = 8
LANES = 128


def pack_kernel(in_ref, out_ref):
    alphas, betas = in_ref.shape
    groups = LANES // alphas
    rows = betas // groups
    for c in range(rows // LANES):
        parts = [in_ref[:, pl.ds(g * rows + c * LANES, LANES)] for g in range(groups)]
        tile = jnp.concatenate(parts, axis=0).astype(jnp.float32)
        out_ref[pl.ds(c * LANES, LANES), :] = tile.T.astype(out_ref.dtype)


def pack_rows(coeffs):
    alphas, betas = coeffs.shape
    return pl.pallas_call(
        pack_kernel,
        out_shape=jax.ShapeDtypeStruct((alphas * betas // LANES, LANES), coeffs.dtype),
        name="pack_rows",
    )(coeffs)


def beta_kernel(chunk, idx_ref, w_ref, alpha_ref, packed_ref, out_ref, table, stage, acc_ref, sems):
    classes, rows = packed_ref.shape[1:3]
    per_class = rows // chunk
    chunks = classes * per_class
    depth = stage.shape[0]
    groups = 8
    width = LANES // groups

    def fetch(c, slot):
        start = pl.multiple_of(lax.rem(c, per_class) * chunk, 16)
        return pltpu.make_async_copy(
            packed_ref.at[:, c // per_class, pl.ds(start, chunk), :], stage.at[slot], sems.at[slot]
        )

    @pl.when(pl.program_id(0) == 0)
    def build_table():
        piece = 32
        part = lax.rem(lax.broadcasted_iota(jnp.int32, (piece, LANES), 1) // width, Y)
        for c in range(depth - 1):
            fetch(c, c).start()

        @pl.loop(0, chunks)
        def _(c):
            slot = lax.rem(c, depth)

            @pl.when(c + depth - 1 < chunks)
            def _():
                fetch(c + depth - 1, lax.rem(c + depth - 1, depth)).start()

            fetch(c, slot).wait()
            first = (c // per_class) * (groups * rows) + lax.rem(c, per_class) * chunk

            @pl.loop(0, chunk // piece)
            def _(s):
                at = pl.multiple_of(s * piece, piece)
                turned = []
                for y in range(Y):
                    shard = stage[slot, y, pl.ds(at, piece), :].astype(jnp.float32)
                    turned.append(pltpu.roll(shard, width * y, 1) if y else shard)
                for g in range(Y):
                    mixed = turned[(Y - 1 - g) % Y]
                    for j in range(Y - 1):
                        mixed = jnp.where(part == j, turned[(j - g) % Y], mixed)
                    for group in (g, g + Y):
                        to = pl.multiple_of(first + group * rows + at, piece)
                        back = (LANES - width * group) % LANES
                        table[pl.ds(to, piece), :] = pltpu.roll(mixed, back, 1) if back else mixed

    slots = w_ref.shape[1]
    block = acc_ref.shape[0]
    lane_row = lax.broadcasted_iota(jnp.int32, (8, LANES), 0)

    @pl.loop(0, block // 8)
    def _(g):
        base = pl.multiple_of(g * 8, 8)
        weights = w_ref[pl.ds(base, 8), :]
        total = jnp.zeros((8, LANES), jnp.float32)
        for q in range(slots):
            picked = None
            for k in range(8):
                source = idx_ref[base + (q * block + k)]
                row = jnp.broadcast_to(table[pl.ds(source, 1), :], (8, LANES))
                picked = row if k == 0 else jnp.where(lane_row == k, row, picked)
            total = total + picked * weights[:, q : q + 1]
        acc_ref[pl.ds(base, 8), :] = total

    alphas = out_ref.shape[0]
    out_ref[...] = (alpha_ref[...] + acc_ref[...].T[:alphas, :]).astype(out_ref.dtype)


def sigma_block(idx, weights, alpha_term, packed, block=128, chunk=768, depth=4):
    targets, slots = weights.shape
    alphas = alpha_term.shape[0]
    _, classes, rows, _ = packed.shape
    betas = classes * rows * 8
    return pl.pallas_call(
        functools.partial(beta_kernel, chunk),
        grid=(targets // block,),
        in_specs=[
            pl.BlockSpec((slots * block,), lambda i: (i,), memory_space=pltpu.SMEM),
            pl.BlockSpec((block, slots), lambda i: (i, 0)),
            pl.BlockSpec((alphas, block), lambda i: (0, i)),
            pl.BlockSpec(memory_space=pl.ANY),
        ],
        out_specs=pl.BlockSpec((alphas, block), lambda i: (0, i)),
        out_shape=jax.ShapeDtypeStruct((alphas, targets), jnp.bfloat16),
        scratch_shapes=[
            pltpu.VMEM((betas, LANES), jnp.float32),
            pltpu.VMEM((depth, Y, chunk, LANES), jnp.bfloat16),
            pltpu.VMEM((block, LANES), jnp.float32),
            pltpu.SemaphoreType.DMA((depth,)),
        ],
        compiler_params=pltpu.CompilerParams(vmem_limit_bytes=56 * 2**20),
        cost_estimate=pl.CostEstimate(
            flops=2 * alphas * targets * slots,
            bytes_accessed=packed.size * 2 + targets * slots * 8 + alphas * targets * 6,
            transcendentals=0,
        ),
        name="sigma_block",
    )(idx, weights, alpha_term, packed)


def per_device(coeffs, alpha_coupling, parent_string_index, excitation_weight):
    own_rows, betas = coeffs.shape
    strings = alpha_coupling.shape[0]
    reps = lax.axis_size("rep")
    cols = lax.axis_size("col")
    parts = reps * Y
    part = betas // parts
    small = part // Z
    along_z = [[y * Z + z for z in range(Z)] for y in range(Y)]
    y_and_col = [[(y * Z + z) * cols + c for y in range(Y) for c in range(cols)] for z in range(Z)]
    row = lax.axis_index("row")
    rep = lax.axis_index("rep")
    mine = (rep * Y + row // Z) * part
    theirs = ((1 - rep) * Y + row // Z) * part

    packed = lax.all_gather(
        pack_rows(coeffs), ("row", "col"), axis=0, axis_index_groups=y_and_col
    ).reshape(Y, cols, -1, LANES)

    half = lax.dynamic_slice_in_dim(coeffs, rep * (Y * part), Y * part, 1)
    pieces = half.reshape(own_rows, Y * Z, small).transpose(1, 0, 2)
    columns = lax.all_to_all(pieces, "row", 0, 0).reshape(strings, small)
    alpha_term = jnp.dot(alpha_coupling, columns, preferred_element_type=jnp.float32)
    alpha_term = alpha_term.reshape(Y, Z, own_rows, small).transpose(1, 0, 2, 3)
    alpha_term = lax.all_to_all(alpha_term, "row", 0, 0, axis_index_groups=along_z)
    alpha_term = alpha_term.transpose(1, 2, 0, 3).reshape(Y * own_rows, part)

    swap = [(0, 1), (1, 0)]

    def all_slots(array):
        own = lax.dynamic_slice_in_dim(array, mine, part, 1)
        other = lax.ppermute(lax.dynamic_slice_in_dim(array, theirs, part, 1), "rep", swap)
        return jnp.concatenate([own, other], axis=0)

    idx = all_slots(parent_string_index)
    idx = idx.reshape(idx.shape[0], part // LANES, LANES).transpose(1, 0, 2).reshape(-1)
    weights = all_slots(excitation_weight).T

    sigma = sigma_block(idx, weights, alpha_term, packed)
    pieces = sigma.reshape(Y, own_rows, part)
    pieces = jnp.concatenate([pieces, pieces], axis=0)
    back = [[r * Y * Z + y * Z + z for r in range(reps) for y in range(Y)] for z in range(Z)]
    done = lax.all_to_all(pieces, ("rep", "row"), 0, 0, axis_index_groups=back, tiled=True)
    return done.reshape(parts, own_rows, part).transpose(1, 0, 2).reshape(own_rows, betas)


def solution(mesh):
    placed = (P("row", "col"), P(), P("rep", "col"), P("rep", "col"))
    return jax.shard_map(
        per_device, mesh=mesh, in_specs=placed, out_specs=P("row", "col"), check_vma=False
    )
```

time: 1250 us -> 253 us (0.20)
  the two profiles are of different devices: /device:TPU:1 before, /device:TPU:32 now
where the time goes in v1:
time: 253 us; the launch traced here: 252 us
  Pallas kernels  109 us (43%)
  blocking collectives  76.5 us (30%)
  waiting for transfers between devices  23 us (9%)
  starting transfers between devices  20.4 us (8%)
  between operations  13.5 us (5%)
  local copies, waits for them, and re-layouts  8.37 us (3%)
    pallas_call x1, Pallas kernels, sigma_block(): pl.pallas_call(functools.partial(beta_kernel, chunk), grid=(targets // bl...  107 us
    all_to_all x1, blocking collectives, per_device(): lax.all_to_all(pieces, ('rep', 'row'), 0, 0, axis_index_groups=back, tile...  43.6 us
    all_to_all x1, blocking collectives, per_device(): columns = lax.all_to_all(pieces, 'row', 0, 0).reshape(strings, small)  33 us
    ppermute x2, waiting for transfers between devices, all_slots(): lax.ppermute(lax.dynamic_slice_in_dim(array, theirs, part, 1), 'rep', swap)  14.6 us
    ppermute x2, starting transfers between devices, all_slots(): lax.ppermute(lax.dynamic_slice_in_dim(array, theirs, part, 1), 'rep', swap)  14.6 us
    all_to_all x1, waiting for transfers between devices, per_device(): lax.all_to_all(alpha_term, 'row', 0, 0, axis_index_groups=along_z)  7.8 us
    all_to_all x1, starting transfers between devices, per_device(): lax.all_to_all(alpha_term, 'row', 0, 0, axis_index_groups=along_z)  5.8 us
  transfers between devices with their start and end apart: 4, of which 4 were waited for; matrix products, arithmetic and copies ran while one was open for 3% of the time, Pallas kernels for 0%

profile of v1, /device:TPU:32, one launch (start us, length us, event | category | flops | bytes accessed | tf_op | source)
XLA Modules:
  0.0 252.5 jit_solution(9653135789883426491)
XLA Ops:
  6.5 0.0 copy-start
  6.5 0.0 all-gather.3.cloned.1.call-start
  6.5 2.0 pack_rows.1
  8.5 0.0 all-gather.3.cloned.1.call-update
  8.6 0.9 constant_dynamic-slice_fusion
  9.5 0.3 reshape.29
  9.8 0.2 copy.24
  10.0 33.0 %all_to_all.15 = bf16[32,16,192]{2,1,0:T(8,128)(2,1)S(1)} all-to-all(bf16[32,16,192]{2,1,0:T(8,128)(2,1)S(1)} %copy.24), channel_id=1, replica_groups=mesh['row'=32,'col'=8,'rep'=2] {'row'}, dimensions={0} | all-to-all | bytes 393216 | tf_op jit(solution)/shard_map/all_to_all | solution.py:157
  42.9 0.0 copy-done
  43.0 0.3 convolution_bitcast_fusion
  43.3 0.2 copy.25
  43.5 0.8 copy.26
  44.3 5.8 %all-to-all-start.1 = ((f32[8,4,16,192]{3,2,1,0:T(8,128)}), f32[8,4,16,192]{3,2,1,0:T(8,128)S(1)}, u32[]{:S(2)}, u32[]{:S(2)}) async-start(f32[8,4,16,192]{3,2,1,0:T(8,128)} %copy.26), calls=%async_computation.1 | async-start | bytes 1048576 | tf_op jit(solution)/shard_map/all_to_all | solution.py:160
  50.1 1.0 constant_dynamic-slice_fusion.4
  51.1 8.2 %collective-permute-start = (s32[16,1536]{1,0:T(8,128)S(1)}, s32[16,1536]{1,0:T(8,128)S(1)}, u32[]{:S(2)}, u32[]{:S(2)}) collective-permute-start(s32[16,1536]{1,0:T(8,128)S(1)} %get-tuple-element.8), channel_id=1, source_target_pairs={{0,1},{1,0},{2,3},{3,2},{4,5},{5,4},{6,7},{7,6},{8,9},{9,8},{10,11... | collective-permute-start | bytes 294920 | tf_op jit(solution)/shard_map/ppermute | solution.py:167
  59.3 1.0 constant_dynamic-slice_fusion.2
  60.3 6.3 %collective-permute-start.1 = (f32[16,1536]{1,0:T(8,128)S(1)}, f32[16,1536]{1,0:T(8,128)S(1)}, u32[]{:S(2)}, u32[]{:S(2)}) collective-permute-start(f32[16,1536]{1,0:T(8,128)S(1)} %get-tuple-element.6), channel_id=1, source_target_pairs={{0,1},{1,0},{2,3},{3,2},{4,5},{5,4},{6,7},{7,6},{8,9},{9,8},{10,11... | collective-permute-start | bytes 294920 | tf_op jit(solution)/shard_map/ppermute | solution.py:167
  66.6 0.3 collective-permute-done
  67.0 0.7 copy.22
  67.7 14.3 %collective-permute-done.1 = f32[16,1536]{1,0:T(8,128)S(1)} collective-permute-done((f32[16,1536]{1,0:T(8,128)S(1)}, f32[16,1536]{1,0:T(8,128)S(1)}, u32[]{:S(2)}, u32[]{:S(2)}) %collective-permute-start.1) | collective-permute-done | bytes 98336 | tf_op jit(solution)/shard_map/ppermute | solution.py:167
  82.0 1.2 copy.23
  83.3 7.8 %all-to-all-done.1 = f32[8,4,16,192]{3,2,1,0:T(8,128)S(1)} async-done(((f32[8,4,16,192]{3,2,1,0:T(8,128)}), f32[8,4,16,192]{3,2,1,0:T(8,128)S(1)}, u32[]{:S(2)}, u32[]{:S(2)}) %all-to-all-start.1) | async-done | bytes 393248 | tf_op jit(solution)/shard_map/all_to_all | solution.py:160
  91.1 0.3 copy.27
  91.4 0.9 reshape.32.alpha_ref
  92.3 0.6 all-gather.3.cloned.1.call-done
  92.9 107.3 %sigma_block.1 = bf16[64,1536]{1,0:T(8,128)(2,1)} custom-call(s32[49152]{0:T(1024)} %bitcast.28, f32[1536,32]{1,0:T(8,128)} %bitcast.21, f32[64,1536]{1,0:T(8,128)} %reshape.32.alpha_ref, bf16[4,8,1536,128]{3,2,1,0:T(8,128)(2,1)} %bitcast.20), custom_call_target="tpu_custom_call" | custom-call | flops 6291456 | bytes 13565952 | tf_op jit(solution)/shard_map/sigma_block/pallas_call | solution.py:109
  200.2 1.1 pad_maximum_fusion
  201.3 43.6 %all_to_all.16 = bf16[8,16,1536]{2,1,0:T(8,128)(2,1)S(1)} all-to-all(bf16[8,16,1536]{2,1,0:T(8,128)(2,1)S(1)} %pad_maximum_fusion), channel_id=1, replica_groups={{0,128,256,384,1,129,257,385},{16,144,272,400,17,145,273,401},{32,160,2..., dimensions={0} | all-to-all | bytes 786432 | tf_op jit(solution)/shard_map/all_to_all | solution.py:178
  244.9 0.8 copy.29
  (3 shorter events, 0.1 us)
Async XLA Ops:
  6.5 36.4 %copy-start = (bf16[512,512]{1,0:T(8,128)(2,1)S(1)}, bf16[512,512]{1,0:T(8,128)(2,1)}, u32[]{:S(2)}) copy-start(bf16[512,512]{1,0:T(8,128)(2,1)} %param.5) | copy-start | bytes 1572868
  6.5 86.4 %all-gather.3.cloned.1.call-start = ((), (), s32[]{:S(2)}) async-start(), calls=%async_computation.3 | async-start | bytes 12976128 | tf_op jit(solution)/shard_map/all_gather | solution.py:151
  44.3 46.7 %all-to-all-start.1 = ((f32[8,4,16,192]{3,2,1,0:T(8,128)}), f32[8,4,16,192]{3,2,1,0:T(8,128)S(1)}, u32[]{:S(2)}, u32[]{:S(2)}) async-start(f32[8,4,16,192]{3,2,1,0:T(8,128)} %copy.26), calls=%async_computation.1 | async-start | bytes 1048576 | tf_op jit(solution)/shard_map/all_to_all | solution.py:160
  51.1 15.8 %collective-permute-start = (s32[16,1536]{1,0:T(8,128)S(1)}, s32[16,1536]{1,0:T(8,128)S(1)}, u32[]{:S(2)}, u32[]{:S(2)}) collective-permute-start(s32[16,1536]{1,0:T(8,128)S(1)} %get-tuple-element.8), channel_id=1, source_target_pairs={{0,1},{1,0},{2,3},{3,2},{4,5},{5,4},{6,7},{7,6},{8,9},{9,8},{10,11... | collective-permute-start | bytes 294920 | tf_op jit(solution)/shard_map/ppermute | solution.py:167
  60.3 21.7 %collective-permute-start.1 = (f32[16,1536]{1,0:T(8,128)S(1)}, f32[16,1536]{1,0:T(8,128)S(1)}, u32[]{:S(2)}, u32[]{:S(2)}) collective-permute-start(f32[16,1536]{1,0:T(8,128)S(1)} %get-tuple-element.6), channel_id=1, source_target_pairs={{0,1},{1,0},{2,3},{3,2},{4,5},{5,4},{6,7},{7,6},{8,9},{9,8},{10,11... | collective-permute-start | bytes 294920 | tf_op jit(solution)/shard_map/ppermute | solution.py:167
Sparse Core Ops, SparseCore 0:
  10.5 82.4 all-gather.2

commit v2 on v1

--- a/solution.py
+++ b/solution.py
@@ -31,13 +31,13 @@
     )(coeffs)
 
 
-def beta_kernel(chunk, idx_ref, w_ref, alpha_ref, packed_ref, out_ref, table, stage, acc_ref, sems):
+def beta_kernel(
+    chunk, idx_ref, w_ref, alpha_ref, packed_ref, out_ref, table, stage, spread, acc_ref, sems
+):
     classes, rows = packed_ref.shape[1:3]
     per_class = rows // chunk
     chunks = classes * per_class
     depth = stage.shape[0]
-    groups = 8
-    width = LANES // groups
 
     def fetch(c, slot):
         start = pl.multiple_of(lax.rem(c, per_class) * chunk, 16)
@@ -47,10 +47,15 @@
 
     @pl.when(pl.program_id(0) == 0)
     def build_table():
-        piece = 32
-        part = lax.rem(lax.broadcasted_iota(jnp.int32, (piece, LANES), 1) // width, Y)
         for c in range(depth - 1):
             fetch(c, c).start()
+        source = lax.broadcasted_iota(jnp.int32, spread.shape, 0)
+        target = (
+            ((source >> 4) & 3) * 128 + ((source >> 6) & 1) * 64 + (source >> 7) * 16 + (source & 15)
+        )
+        column = lax.broadcasted_iota(jnp.int32, spread.shape, 1)
+        spread[...] = jnp.where(target == column, 1.0, 0.0).astype(spread.dtype)
+        piece = 256
 
         @pl.loop(0, chunks)
         def _(c):
@@ -61,27 +66,20 @@
                 fetch(c + depth - 1, lax.rem(c + depth - 1, depth)).start()
 
             fetch(c, slot).wait()
-            first = (c // per_class) * (groups * rows) + lax.rem(c, per_class) * chunk
+            first = (c // per_class) * (Y * rows) + lax.rem(c, per_class) * chunk
+            for at in range(0, chunk, piece):
+                shards = [stage[slot, y, pl.ds(at, piece), :] for y in range(Y)]
+                mixed = jnp.dot(
+                    jnp.concatenate(shards, axis=1), spread[...], preferred_element_type=jnp.float32
+                )
+                for g in range(Y):
+                    to = pl.multiple_of(first + (g * rows + at), 8)
+                    table[pl.ds(to, piece), :] = mixed[:, g * LANES : (g + 1) * LANES]
 
-            @pl.loop(0, chunk // piece)
-            def _(s):
-                at = pl.multiple_of(s * piece, piece)
-                turned = []
-                for y in range(Y):
-                    shard = stage[slot, y, pl.ds(at, piece), :].astype(jnp.float32)
-                    turned.append(pltpu.roll(shard, width * y, 1) if y else shard)
-                for g in range(Y):
-                    mixed = turned[(Y - 1 - g) % Y]
-                    for j in range(Y - 1):
-                        mixed = jnp.where(part == j, turned[(j - g) % Y], mixed)
-                    for group in (g, g + Y):
-                        to = pl.multiple_of(first + group * rows + at, piece)
-                        back = (LANES - width * group) % LANES
-                        table[pl.ds(to, piece), :] = pltpu.roll(mixed, back, 1) if back else mixed
-
-    slots = w_ref.shape[1]
+    slots = w_ref.shape[1] // 2
     block = acc_ref.shape[0]
     lane_row = lax.broadcasted_iota(jnp.int32, (8, LANES), 0)
+    low_lane = lax.broadcasted_iota(jnp.int32, (8, LANES), 1) < LANES // 2
 
     @pl.loop(0, block // 8)
     def _(g):
@@ -94,23 +92,27 @@
                 source = idx_ref[base + (q * block + k)]
                 row = jnp.broadcast_to(table[pl.ds(source, 1), :], (8, LANES))
                 picked = row if k == 0 else jnp.where(lane_row == k, row, picked)
-            total = total + picked * weights[:, q : q + 1]
+            low = jnp.broadcast_to(weights[:, q : q + 1], (8, LANES))
+            high = jnp.broadcast_to(weights[:, slots + q : slots + q + 1], (8, LANES))
+            total = total + picked * jnp.where(low_lane, low, high)
         acc_ref[pl.ds(base, 8), :] = total
 
     alphas = out_ref.shape[0]
-    out_ref[...] = (alpha_ref[...] + acc_ref[...].T[:alphas, :]).astype(out_ref.dtype)
+    turned = acc_ref[...].T
+    beta_term = turned[:alphas, :] + turned[alphas:, :]
+    out_ref[...] = (alpha_ref[...] + beta_term).astype(out_ref.dtype)
 
 
 def sigma_block(idx, weights, alpha_term, packed, block=128, chunk=768, depth=4):
     targets, slots = weights.shape
     alphas = alpha_term.shape[0]
     _, classes, rows, _ = packed.shape
-    betas = classes * rows * 8
+    pairs = classes * rows * Y
     return pl.pallas_call(
         functools.partial(beta_kernel, chunk),
         grid=(targets // block,),
         in_specs=[
-            pl.BlockSpec((slots * block,), lambda i: (i,), memory_space=pltpu.SMEM),
+            pl.BlockSpec((slots // 2 * block,), lambda i: (i,), memory_space=pltpu.SMEM),
             pl.BlockSpec((block, slots), lambda i: (i, 0)),
             pl.BlockSpec((alphas, block), lambda i: (0, i)),
             pl.BlockSpec(memory_space=pl.ANY),
@@ -118,14 +120,15 @@
         out_specs=pl.BlockSpec((alphas, block), lambda i: (0, i)),
         out_shape=jax.ShapeDtypeStruct((alphas, targets), jnp.bfloat16),
         scratch_shapes=[
-            pltpu.VMEM((betas, LANES), jnp.float32),
+            pltpu.VMEM((pairs, LANES), jnp.float32),
             pltpu.VMEM((depth, Y, chunk, LANES), jnp.bfloat16),
+            pltpu.VMEM((Y * LANES, Y * LANES), jnp.bfloat16),
             pltpu.VMEM((block, LANES), jnp.float32),
             pltpu.SemaphoreType.DMA((depth,)),
         ],
         compiler_params=pltpu.CompilerParams(vmem_limit_bytes=56 * 2**20),
         cost_estimate=pl.CostEstimate(
-            flops=2 * alphas * targets * slots,
+            flops=2 * alphas * targets * slots + 2 * pairs * LANES * Y * LANES,
             bytes_accessed=packed.size * 2 + targets * slots * 8 + alphas * targets * 6,
             transcendentals=0,
         ),
@@ -168,8 +171,14 @@
         return jnp.concatenate([own, other], axis=0)
 
     idx = all_slots(parent_string_index)
+    halves = idx // (betas // 2)
+    idx = idx - ((halves + 1) // 2) * (betas // 2)
     idx = idx.reshape(idx.shape[0], part // LANES, LANES).transpose(1, 0, 2).reshape(-1)
-    weights = all_slots(excitation_weight).T
+    weights = all_slots(excitation_weight)
+    upper = halves % 2 == 1
+    weights = jnp.concatenate(
+        [jnp.where(upper, 0.0, weights), jnp.where(upper, weights, 0.0)], axis=0
+    ).T
 
     sigma = sigma_block(idx, weights, alpha_term, packed)
     pieces = sigma.reshape(Y, own_rows, part)

time: 253 us -> 202 us (0.80)
  Pallas kernels: 109 us -> 57.2 us
  blocking collectives: 76.5 us -> 42 us
  starting transfers between devices: 20.4 us -> 38.4 us
  waiting for transfers between devices: 23 us -> 37.6 us
  other arithmetic: 1.09 us -> 3.66 us
    pallas_call x1, Pallas kernels: 107 us -> 55.3 us  [sigma_block(): pl.pallas_call(functools.partial(beta_kernel, chunk), grid=(targets // bl...]
    all_to_all x1 -> x0, blocking collectives: 33 us -> none  [per_device(): columns = lax.all_to_all(pieces, 'row', 0, 0).reshape(strings, small)]
    all_to_all x1, waiting for transfers between devices: 7.8 us -> 22.1 us  [per_device(): lax.all_to_all(alpha_term, 'row', 0, 0, axis_index_groups=along_z)]
    all_to_all x0 -> x1, starting transfers between devices: none -> 8.81 us  [per_device(): columns = lax.all_to_all(pieces, 'row', 0, 0).reshape(strings, small)]
    ppermute x2, starting transfers between devices: 14.6 us -> 21.2 us  [all_slots(): lax.ppermute(lax.dynamic_slice_in_dim(array, theirs, part, 1), 'rep', swap)]
    all_to_all x0 -> x1, waiting for transfers between devices: none -> 5.52 us  [per_device(): columns = lax.all_to_all(pieces, 'row', 0, 0).reshape(strings, small)]
    ppermute x2, waiting for transfers between devices: 14.6 us -> 9.95 us  [all_slots(): lax.ppermute(lax.dynamic_slice_in_dim(array, theirs, part, 1), 'rep', swap)]
    all_to_all x1, starting transfers between devices: 5.8 us -> 8.46 us  [per_device(): lax.all_to_all(alpha_term, 'row', 0, 0, axis_index_groups=along_z)]
  transfers between devices with their start and end apart: 4 -> 5, of which waited for: 4 -> 3; matrix products, arithmetic and copies ran while one was open for 3% -> 5% of each run, Pallas kernels for 0% -> 0%
where the time goes in v2:
time: 202 us; the launch traced here: 201 us
  Pallas kernels  57.2 us (28%)
  blocking collectives  42 us (21%)
  starting transfers between devices  38.4 us (19%)
  waiting for transfers between devices  37.6 us (19%)
  between operations  13.6 us (7%)
  local copies, waits for them, and re-layouts  8.43 us (4%)
  other arithmetic  3.66 us (2%)
    pallas_call x1, Pallas kernels, sigma_block(): pl.pallas_call(functools.partial(beta_kernel, chunk), grid=(targets // bl...  55.3 us
    all_to_all x1, blocking collectives, per_device(): lax.all_to_all(pieces, ('rep', 'row'), 0, 0, axis_index_groups=back, tile...  42 us
    all_to_all x1, waiting for transfers between devices, per_device(): lax.all_to_all(alpha_term, 'row', 0, 0, axis_index_groups=along_z)  22.1 us
    ppermute x2, starting transfers between devices, all_slots(): lax.ppermute(lax.dynamic_slice_in_dim(array, theirs, part, 1), 'rep', swap)  21.2 us
    ppermute x2, waiting for transfers between devices, all_slots(): lax.ppermute(lax.dynamic_slice_in_dim(array, theirs, part, 1), 'rep', swap)  9.95 us
    all_to_all x1, starting transfers between devices, per_device(): columns = lax.all_to_all(pieces, 'row', 0, 0).reshape(strings, small)  8.81 us
    all_to_all x1, starting transfers between devices, per_device(): lax.all_to_all(alpha_term, 'row', 0, 0, axis_index_groups=along_z)  8.46 us
    all_to_all x1, waiting for transfers between devices, per_device(): columns = lax.all_to_all(pieces, 'row', 0, 0).reshape(strings, small)  5.52 us
  transfers between devices with their start and end apart: 5, of which 3 were waited for; matrix products, arithmetic and copies ran while one was open for 5% of the time, Pallas kernels for 0%

profile of v2, /device:TPU:32, one launch (start us, length us, event | category | flops | bytes accessed | tf_op | source)
XLA Modules:
  0.0 201.2 jit_solution(1967845175050952885)
XLA Ops:
  6.5 0.0 copy-start
  6.5 0.0 all-gather.3.cloned.1.call-start
  6.5 2.0 pack_rows.1
  8.5 0.0 all-gather.3.cloned.1.call-update
  8.6 1.0 constant_dynamic-slice_fusion.2
  9.5 14.8 %collective-permute-start.1 = (f32[16,1536]{1,0:T(8,128)S(1)}, f32[16,1536]{1,0:T(8,128)S(1)}, u32[]{:S(2)}, u32[]{:S(2)}) collective-permute-start(f32[16,1536]{1,0:T(8,128)S(1)} %get-tuple-element.8), channel_id=1, source_target_pairs={{0,1},{1,0},{2,3},{3,2},{4,5},{5,4},{6,7},{7,6},{8,9},{9,8},{10,11... | collective-permute-start | bytes 294920 | tf_op jit(solution)/shard_map/ppermute | solution.py:170
  24.4 0.9 constant_dynamic-slice_fusion
  25.3 0.3 reshape.28
  25.6 0.9 copy.47
  26.5 8.8 %all-to-all-start = ((bf16[32,16,192]{2,1,0:T(8,128)(2,1)}), bf16[32,16,192]{2,1,0:T(8,128)(2,1)S(1)}, u32[]{:S(2)}, u32[]{:S(2)}) async-start(bf16[32,16,192]{2,1,0:T(8,128)(2,1)} %copy.47), calls=%async_computation | async-start | bytes 524288 | tf_op jit(solution)/shard_map/all_to_all | solution.py:160
  35.3 1.0 constant_dynamic-slice_fusion.3
  36.3 6.3 %collective-permute-start = (s32[16,1536]{1,0:T(8,128)S(1)}, s32[16,1536]{1,0:T(8,128)S(1)}, u32[]{:S(2)}, u32[]{:S(2)}) collective-permute-start(s32[16,1536]{1,0:T(8,128)S(1)} %get-tuple-element.9), channel_id=1, source_target_pairs={{0,1},{1,0},{2,3},{3,2},{4,5},{5,4},{6,7},{7,6},{8,9},{9,8},{10,11... | collective-permute-start | bytes 294920 | tf_op jit(solution)/shard_map/ppermute | solution.py:170
  42.7 9.9 %collective-permute-done = s32[16,1536]{1,0:T(8,128)S(1)} collective-permute-done((s32[16,1536]{1,0:T(8,128)S(1)}, s32[16,1536]{1,0:T(8,128)S(1)}, u32[]{:S(2)}, u32[]{:S(2)}) %collective-permute-start) | collective-permute-done | bytes 98336 | tf_op jit(solution)/shard_map/ppermute | solution.py:170
  52.7 0.3 fusion.7
  53.0 5.5 %all-to-all-done = bf16[32,16,192]{2,1,0:T(8,128)(2,1)S(1)} async-done(((bf16[32,16,192]{2,1,0:T(8,128)(2,1)}), bf16[32,16,192]{2,1,0:T(8,128)(2,1)S(1)}, u32[]{:S(2)}, u32[]{:S(2)}) %all-to-all-start) | async-done | bytes 196640 | tf_op jit(solution)/shard_map/all_to_all | solution.py:160
  58.5 0.0 copy-done
  58.6 0.3 convolution_bitcast_fusion
  58.9 0.2 copy.48
  59.1 0.8 copy.49
  59.9 8.5 %all-to-all-start.1 = ((f32[8,4,16,192]{3,2,1,0:T(8,128)}), f32[8,4,16,192]{3,2,1,0:T(8,128)S(1)}, u32[]{:S(2)}, u32[]{:S(2)}) async-start(f32[8,4,16,192]{3,2,1,0:T(8,128)} %copy.49), calls=%async_computation.1 | async-start | bytes 1048576 | tf_op jit(solution)/shard_map/all_to_all | solution.py:163
  68.4 0.0 collective-permute-done.1
  68.4 0.3 copy.45
  68.7 0.3 copy.42
  69.0 0.8 copy.41
  69.7 0.9 broadcast_select_fusion.1
  70.6 0.1 broadcast_select_fusion
  70.7 1.2 maximum_bitcast_fusion.w_ref
  72.0 22.1 %all-to-all-done.1 = f32[8,4,16,192]{3,2,1,0:T(8,128)S(1)} async-done(((f32[8,4,16,192]{3,2,1,0:T(8,128)}), f32[8,4,16,192]{3,2,1,0:T(8,128)S(1)}, u32[]{:S(2)}, u32[]{:S(2)}) %all-to-all-start.1) | async-done | bytes 393248 | tf_op jit(solution)/shard_map/all_to_all | solution.py:163
  94.1 0.3 copy.50
  94.4 0.9 reshape.31.alpha_ref
  95.3 0.0 all-gather.3.cloned.1.call-done
  95.3 55.3 %sigma_block.1 = bf16[64,1536]{1,0:T(8,128)(2,1)} custom-call(s32[49152]{0:T(1024)} %bitcast.27, f32[1536,64]{1,0:T(8,128)} %maximum_bitcast_fusion.w_ref, f32[64,1536]{1,0:T(8,128)} %reshape.31.alpha_ref, bf16[4,8,1536,128]{3,2,1,0:T(8,128)(2,1)} %bitcast.29), custom_call_target="tpu_custom_call" | custom-call | flops 6455033856 | bytes 13959168 | tf_op jit(solution)/shard_map/sigma_block/pallas_call | solution.py:111
  150.6 1.1 pad_maximum_fusion
  151.6 42.0 %all_to_all.15 = bf16[8,16,1536]{2,1,0:T(8,128)(2,1)S(1)} all-to-all(bf16[8,16,1536]{2,1,0:T(8,128)(2,1)S(1)} %pad_maximum_fusion), channel_id=1, replica_groups={{0,128,256,384,1,129,257,385},{16,144,272,400,17,145,273,401},{32,160,2..., dimensions={0} | all-to-all | bytes 786432 | tf_op jit(solution)/shard_map/all_to_all | solution.py:187
  193.6 0.8 copy.52
  (6 shorter events, 0.1 us)
Async XLA Ops:
  6.5 52.0 %copy-start = (bf16[512,512]{1,0:T(8,128)(2,1)S(1)}, bf16[512,512]{1,0:T(8,128)(2,1)}, u32[]{:S(2)}) copy-start(bf16[512,512]{1,0:T(8,128)(2,1)} %param.5) | copy-start | bytes 1572868
  6.5 88.8 %all-gather.3.cloned.1.call-start = ((), (), s32[]{:S(2)}) async-start(), calls=%async_computation.3 | async-start | bytes 12976128 | tf_op jit(solution)/shard_map/all_gather | solution.py:154
  9.5 58.9 %collective-permute-start.1 = (f32[16,1536]{1,0:T(8,128)S(1)}, f32[16,1536]{1,0:T(8,128)S(1)}, u32[]{:S(2)}, u32[]{:S(2)}) collective-permute-start(f32[16,1536]{1,0:T(8,128)S(1)} %get-tuple-element.8), channel_id=1, source_target_pairs={{0,1},{1,0},{2,3},{3,2},{4,5},{5,4},{6,7},{7,6},{8,9},{9,8},{10,11... | collective-permute-start | bytes 294920 | tf_op jit(solution)/shard_map/ppermute | solution.py:170
  26.5 32.1 %all-to-all-start = ((bf16[32,16,192]{2,1,0:T(8,128)(2,1)}), bf16[32,16,192]{2,1,0:T(8,128)(2,1)S(1)}, u32[]{:S(2)}, u32[]{:S(2)}) async-start(bf16[32,16,192]{2,1,0:T(8,128)(2,1)} %copy.47), calls=%async_computation | async-start | bytes 524288 | tf_op jit(solution)/shard_map/all_to_all | solution.py:160
  36.3 16.3 %collective-permute-start = (s32[16,1536]{1,0:T(8,128)S(1)}, s32[16,1536]{1,0:T(8,128)S(1)}, u32[]{:S(2)}, u32[]{:S(2)}) collective-permute-start(s32[16,1536]{1,0:T(8,128)S(1)} %get-tuple-element.9), channel_id=1, source_target_pairs={{0,1},{1,0},{2,3},{3,2},{4,5},{5,4},{6,7},{7,6},{8,9},{9,8},{10,11... | collective-permute-start | bytes 294920 | tf_op jit(solution)/shard_map/ppermute | solution.py:170
  59.9 34.1 %all-to-all-start.1 = ((f32[8,4,16,192]{3,2,1,0:T(8,128)}), f32[8,4,16,192]{3,2,1,0:T(8,128)S(1)}, u32[]{:S(2)}, u32[]{:S(2)}) async-start(f32[8,4,16,192]{3,2,1,0:T(8,128)} %copy.49), calls=%async_computation.1 | async-start | bytes 1048576 | tf_op jit(solution)/shard_map/all_to_all | solution.py:163
Sparse Core Ops, SparseCore 0:
  10.5 83.1 all-gather.2

commit v3 on v2

--- a/solution.py
+++ b/solution.py
@@ -32,12 +32,17 @@
 
 
 def beta_kernel(
-    chunk, idx_ref, w_ref, alpha_ref, packed_ref, out_ref, table, stage, spread, acc_ref, sems
+    chunk,
+    idx_ref, w_ref, alpha_ref, packed_ref, out_ref,
+    table, stage, spread, acc_ref, near, sems, near_sems,
 ):
     classes, rows = packed_ref.shape[1:3]
     per_class = rows // chunk
     chunks = classes * per_class
     depth = stage.shape[0]
+    buffers, batch, slots = near.shape
+    targets = w_ref.shape[0]
+    rounds = targets // (buffers * batch)
 
     def fetch(c, slot):
         start = pl.multiple_of(lax.rem(c, per_class) * chunk, 16)
@@ -45,86 +50,101 @@
             packed_ref.at[:, c // per_class, pl.ds(start, chunk), :], stage.at[slot], sems.at[slot]
         )
 
-    @pl.when(pl.program_id(0) == 0)
-    def build_table():
-        for c in range(depth - 1):
-            fetch(c, c).start()
-        source = lax.broadcasted_iota(jnp.int32, spread.shape, 0)
-        target = (
-            ((source >> 4) & 3) * 128 + ((source >> 6) & 1) * 64 + (source >> 7) * 16 + (source & 15)
+    def bring(r, b):
+        start = pl.multiple_of((r * buffers + b) * batch, batch)
+        return pltpu.make_async_copy(
+            idx_ref.at[pl.ds(start, batch), :], near.at[b], near_sems.at[b]
         )
-        column = lax.broadcasted_iota(jnp.int32, spread.shape, 1)
-        spread[...] = jnp.where(target == column, 1.0, 0.0).astype(spread.dtype)
-        piece = 256
-
-        @pl.loop(0, chunks)
-        def _(c):
-            slot = lax.rem(c, depth)
-
-            @pl.when(c + depth - 1 < chunks)
-            def _():
-                fetch(c + depth - 1, lax.rem(c + depth - 1, depth)).start()
-
-            fetch(c, slot).wait()
-            first = (c // per_class) * (Y * rows) + lax.rem(c, per_class) * chunk
-            for at in range(0, chunk, piece):
-                shards = [stage[slot, y, pl.ds(at, piece), :] for y in range(Y)]
-                mixed = jnp.dot(
-                    jnp.concatenate(shards, axis=1), spread[...], preferred_element_type=jnp.float32
-                )
-                for g in range(Y):
-                    to = pl.multiple_of(first + (g * rows + at), 8)
-                    table[pl.ds(to, piece), :] = mixed[:, g * LANES : (g + 1) * LANES]
-
-    slots = w_ref.shape[1] // 2
-    block = acc_ref.shape[0]
+
+    for c in range(depth - 1):
+        fetch(c, c).start()
+    for b in range(buffers):
+        bring(0, b).start()
+
+    source = lax.broadcasted_iota(jnp.int32, spread.shape, 0)
+    target = (
+        ((source >> 4) & 3) * 128 + ((source >> 6) & 1) * 64 + (source >> 7) * 16 + (source & 15)
+    )
+    column = lax.broadcasted_iota(jnp.int32, spread.shape, 1)
+    spread[...] = jnp.where(target == column, 1.0, 0.0).astype(spread.dtype)
+    piece = 256
+
+    @pl.loop(0, chunks)
+    def _(c):
+        slot = lax.rem(c, depth)
+
+        @pl.when(c + depth - 1 < chunks)
+        def _():
+            fetch(c + depth - 1, lax.rem(c + depth - 1, depth)).start()
+
+        fetch(c, slot).wait()
+        first = (c // per_class) * (Y * rows) + lax.rem(c, per_class) * chunk
+        for at in range(0, chunk, piece):
+            shards = [stage[slot, y, pl.ds(at, piece), :] for y in range(Y)]
+            mixed = jnp.dot(
+                jnp.concatenate(shards, axis=1), spread[...], preferred_element_type=jnp.float32
+            )
+            for g in range(Y):
+                to = pl.multiple_of(first + (g * rows + at), 8)
+                table[pl.ds(to, piece), :] = mixed[:, g * LANES : (g + 1) * LANES]
+
     lane_row = lax.broadcasted_iota(jnp.int32, (8, LANES), 0)
     low_lane = lax.broadcasted_iota(jnp.int32, (8, LANES), 1) < LANES // 2
 
-    @pl.loop(0, block // 8)
-    def _(g):
-        base = pl.multiple_of(g * 8, 8)
-        weights = w_ref[pl.ds(base, 8), :]
-        total = jnp.zeros((8, LANES), jnp.float32)
-        for q in range(slots):
-            picked = None
-            for k in range(8):
-                source = idx_ref[base + (q * block + k)]
-                row = jnp.broadcast_to(table[pl.ds(source, 1), :], (8, LANES))
-                picked = row if k == 0 else jnp.where(lane_row == k, row, picked)
-            low = jnp.broadcast_to(weights[:, q : q + 1], (8, LANES))
-            high = jnp.broadcast_to(weights[:, slots + q : slots + q + 1], (8, LANES))
-            total = total + picked * jnp.where(low_lane, low, high)
-        acc_ref[pl.ds(base, 8), :] = total
+    @pl.loop(0, rounds)
+    def _(r):
+        for b in range(buffers):
+            bring(r, b).wait()
+            for g in range(0, batch, 8):
+                base = pl.multiple_of((r * buffers + b) * batch + g, 8)
+                weights = w_ref[pl.ds(base, 8), :]
+                total = jnp.zeros((8, LANES), jnp.float32)
+                for q in range(slots):
+                    picked = None
+                    for k in range(8):
+                        row = table[pl.ds(near[b, g + k, q], 1), :]
+                        row = jnp.broadcast_to(row, (8, LANES))
+                        picked = row if k == 0 else jnp.where(lane_row == k, row, picked)
+                    low = jnp.broadcast_to(weights[:, q : q + 1], (8, LANES))
+                    high = jnp.broadcast_to(weights[:, slots + q : slots + q + 1], (8, LANES))
+                    total = total + picked * jnp.where(low_lane, low, high)
+                acc_ref[pl.ds(base, 8), :] = total
+
+            @pl.when(r + 1 < rounds)
+            def _():
+                bring(r + 1, b).start()
 
     alphas = out_ref.shape[0]
-    turned = acc_ref[...].T
-    beta_term = turned[:alphas, :] + turned[alphas:, :]
-    out_ref[...] = (alpha_ref[...] + beta_term).astype(out_ref.dtype)
-
-
-def sigma_block(idx, weights, alpha_term, packed, block=128, chunk=768, depth=4):
-    targets, slots = weights.shape
+    for at in range(0, targets, LANES):
+        turned = acc_ref[pl.ds(at, LANES), :].T
+        beta_term = turned[:alphas, :] + turned[alphas:, :]
+        total = alpha_ref[:, pl.ds(at, LANES)] + beta_term
+        out_ref[:, pl.ds(at, LANES)] = total.astype(out_ref.dtype)
+
+
+def sigma_block(idx, weights, alpha_term, packed, chunk=768, depth=4, buffers=4, batch=16):
+    targets, slots = idx.shape
     alphas = alpha_term.shape[0]
     _, classes, rows, _ = packed.shape
     pairs = classes * rows * Y
     return pl.pallas_call(
         functools.partial(beta_kernel, chunk),
-        grid=(targets // block,),
         in_specs=[
-            pl.BlockSpec((slots // 2 * block,), lambda i: (i,), memory_space=pltpu.SMEM),
-            pl.BlockSpec((block, slots), lambda i: (i, 0)),
-            pl.BlockSpec((alphas, block), lambda i: (0, i)),
+            pl.BlockSpec(memory_space=pl.ANY),
+            pl.BlockSpec(memory_space=pltpu.VMEM),
+            pl.BlockSpec(memory_space=pltpu.VMEM),
             pl.BlockSpec(memory_space=pl.ANY),
         ],
-        out_specs=pl.BlockSpec((alphas, block), lambda i: (0, i)),
+        out_specs=pl.BlockSpec(memory_space=pltpu.VMEM),
         out_shape=jax.ShapeDtypeStruct((alphas, targets), jnp.bfloat16),
         scratch_shapes=[
             pltpu.VMEM((pairs, LANES), jnp.float32),
             pltpu.VMEM((depth, Y, chunk, LANES), jnp.bfloat16),
             pltpu.VMEM((Y * LANES, Y * LANES), jnp.bfloat16),
-            pltpu.VMEM((block, LANES), jnp.float32),
+            pltpu.VMEM((targets, LANES), jnp.float32),
+            pltpu.SMEM((buffers, batch, slots), jnp.int32),
             pltpu.SemaphoreType.DMA((depth,)),
+            pltpu.SemaphoreType.DMA((buffers,)),
         ],
         compiler_params=pltpu.CompilerParams(vmem_limit_bytes=56 * 2**20),
         cost_estimate=pl.CostEstimate(
@@ -173,7 +193,7 @@
     idx = all_slots(parent_string_index)
     halves = idx // (betas // 2)
     idx = idx - ((halves + 1) // 2) * (betas // 2)
-    idx = idx.reshape(idx.shape[0], part // LANES, LANES).transpose(1, 0, 2).reshape(-1)
+    idx = idx.T
     weights = all_slots(excitation_weight)
     upper = halves % 2 == 1
     weights = jnp.concatenate(

time: 202 us -> 192 us (0.950)
  Pallas kernels: 57.2 us -> 48.7 us
  starting transfers between devices: 38.4 us -> 41.5 us
  blocking collectives: 42 us -> 39.3 us
    pallas_call x1, Pallas kernels: 55.3 us -> 46.7 us  [sigma_block(): pl.pallas_call(functools.partial(beta_kernel, chunk), in_specs=[pl.BlockS...]
    all_to_all x1, starting transfers between devices: 8.81 us -> 15.4 us  [per_device(): columns = lax.all_to_all(pieces, 'row', 0, 0).reshape(strings, small)]
    ppermute x2, starting transfers between devices: 21.2 us -> 14.6 us  [all_slots(): lax.ppermute(lax.dynamic_slice_in_dim(array, theirs, part, 1), 'rep', swap)]
    all_to_all x1, waiting for transfers between devices: 5.52 us -> 0.01 us  [per_device(): columns = lax.all_to_all(pieces, 'row', 0, 0).reshape(strings, small)]
    ppermute x2, waiting for transfers between devices: 9.95 us -> 13.7 us  [all_slots(): lax.ppermute(lax.dynamic_slice_in_dim(array, theirs, part, 1), 'rep', swap)]
    all_to_all x1, starting transfers between devices: 8.46 us -> 11.5 us  [per_device(): lax.all_to_all(alpha_term, 'row', 0, 0, axis_index_groups=along_z)]
    all_to_all x1, blocking collectives: 42 us -> 39.3 us  [per_device(): lax.all_to_all(pieces, ('rep', 'row'), 0, 0, axis_index_groups=back, tile...]
  transfers between devices with their start and end apart: 5 -> 5, of which waited for: 3 -> 3; matrix products, arithmetic and copies ran while one was open for 5% -> 6% of each run, Pallas kernels for 0% -> 0%
where the time goes in v3:
time: 192 us
  Pallas kernels  48.7 us (25%)
  starting transfers between devices  41.5 us (22%)
  blocking collectives  39.3 us (20%)
  waiting for transfers between devices  35.6 us (19%)
  between operations  13.5 us (7%)
  local copies, waits for them, and re-layouts  7.59 us (4%)
  other arithmetic  5.22 us (3%)
    pallas_call x1, Pallas kernels, sigma_block(): pl.pallas_call(functools.partial(beta_kernel, chunk), in_specs=[pl.BlockS...  46.7 us
    all_to_all x1, blocking collectives, per_device(): lax.all_to_all(pieces, ('rep', 'row'), 0, 0, axis_index_groups=back, tile...  39.3 us
    all_to_all x1, waiting for transfers between devices, per_device(): lax.all_to_all(alpha_term, 'row', 0, 0, axis_index_groups=along_z)  21.9 us
    all_to_all x1, starting transfers between devices, per_device(): columns = lax.all_to_all(pieces, 'row', 0, 0).reshape(strings, small)  15.4 us
    ppermute x2, starting transfers between devices, all_slots(): lax.ppermute(lax.dynamic_slice_in_dim(array, theirs, part, 1), 'rep', swap)  14.6 us
    ppermute x2, waiting for transfers between devices, all_slots(): lax.ppermute(lax.dynamic_slice_in_dim(array, theirs, part, 1), 'rep', swap)  13.7 us
    all_to_all x1, starting transfers between devices, per_device(): lax.all_to_all(alpha_term, 'row', 0, 0, axis_index_groups=along_z)  11.5 us
  transfers between devices with their start and end apart: 5, of which 3 were waited for; matrix products, arithmetic and copies ran while one was open for 6% of the time, Pallas kernels for 0%

profile of v3, /device:TPU:32, one launch (start us, length us, event | category | flops | bytes accessed | tf_op | source)
XLA Modules:
  0.0 191.8 jit_solution(18377557901976555094)
XLA Ops:
  6.5 0.0 copy-start
  6.5 0.0 all-gather.3.cloned.1.call-start
  6.5 2.0 %pack_rows.1 = bf16[1536,128]{1,0:T(8,128)(2,1)} custom-call(bf16[16,12288]{1,0:T(8,128)(2,1)} %in_ref.1), custom_call_target="tpu_custom_call" | custom-call | tf_op jit(solution)/shard_map/pack_rows/pallas_call | solution.py:27
  8.5 0.0 all-gather.3.cloned.1.call-update
  8.6 0.9 constant_dynamic-slice_fusion
  9.5 0.3 reshape.21
  9.8 0.9 copy.43
  10.7 15.4 %all-to-all-start = ((bf16[32,16,192]{2,1,0:T(8,128)(2,1)}), bf16[32,16,192]{2,1,0:T(8,128)(2,1)S(1)}, u32[]{:S(2)}, u32[]{:S(2)}) async-start(bf16[32,16,192]{2,1,0:T(8,128)(2,1)} %copy.43), calls=%async_computation | async-start | bytes 524288 | tf_op jit(solution)/shard_map/all_to_all | solution.py:180
  26.1 1.0 constant_dynamic-slice_fusion.2
  27.1 8.2 %collective-permute-start.1 = (f32[16,1536]{1,0:T(8,128)S(1)}, f32[16,1536]{1,0:T(8,128)S(1)}, u32[]{:S(2)}, u32[]{:S(2)}) collective-permute-start(f32[16,1536]{1,0:T(8,128)S(1)} %get-tuple-element.8), channel_id=1, source_target_pairs={{0,1},{1,0},{2,3},{3,2},{4,5},{5,4},{6,7},{7,6},{8,9},{9,8},{10,11... | collective-permute-start | bytes 294920 | tf_op jit(solution)/shard_map/ppermute | solution.py:190
  35.3 1.0 constant_dynamic-slice_fusion.4
  36.3 6.3 %collective-permute-start = (s32[16,1536]{1,0:T(8,128)S(1)}, s32[16,1536]{1,0:T(8,128)S(1)}, u32[]{:S(2)}, u32[]{:S(2)}) collective-permute-start(s32[16,1536]{1,0:T(8,128)S(1)} %get-tuple-element.10), channel_id=1, source_target_pairs={{0,1},{1,0},{2,3},{3,2},{4,5},{5,4},{6,7},{7,6},{8,9},{9,8},{10,11... | collective-permute-start | bytes 294920 | tf_op jit(solution)/shard_map/ppermute | solution.py:190
  42.6 0.8 collective-permute-done.1
  43.5 0.3 copy.41
  43.8 12.9 %collective-permute-done = s32[16,1536]{1,0:T(8,128)S(1)} collective-permute-done((s32[16,1536]{1,0:T(8,128)S(1)}, s32[16,1536]{1,0:T(8,128)S(1)}, u32[]{:S(2)}, u32[]{:S(2)}) %collective-permute-start) | collective-permute-done | bytes 98336 | tf_op jit(solution)/shard_map/ppermute | solution.py:190
  56.7 0.3 copy.40
  56.9 0.0 all-to-all-done
  56.9 0.0 copy-done
  57.0 0.3 convolution_bitcast_fusion
  57.3 0.2 copy.44
  57.5 0.8 copy.45
  58.3 11.5 %all-to-all-start.1 = ((f32[8,4,16,192]{3,2,1,0:T(8,128)}), f32[8,4,16,192]{3,2,1,0:T(8,128)S(1)}, u32[]{:S(2)}, u32[]{:S(2)}) async-start(f32[8,4,16,192]{3,2,1,0:T(8,128)} %copy.45), calls=%async_computation.1 | async-start | bytes 1048576 | tf_op jit(solution)/shard_map/all_to_all | solution.py:183
  69.8 0.9 broadcast_select_fusion.1
  70.7 0.1 broadcast_select_fusion
  70.8 1.2 maximum_bitcast_fusion.w_ref
  72.0 2.0 %fusion.3.idx_ref = s32[1536,32]{1,0:T(8,128)} fusion(s32[32,1536]{0,1:T(8,128)S(1)} %copy.40), kind=kLoop, calls=%fused_computation.12 | loop fusion | flops 1277952 | bytes 393216 | tf_op jit(solution)/shard_map/transpose | solution.py:196
  74.0 21.9 %all-to-all-done.1 = f32[8,4,16,192]{3,2,1,0:T(8,128)S(1)} async-done(((f32[8,4,16,192]{3,2,1,0:T(8,128)}), f32[8,4,16,192]{3,2,1,0:T(8,128)S(1)}, u32[]{:S(2)}, u32[]{:S(2)}) %all-to-all-start.1) | async-done | bytes 393248 | tf_op jit(solution)/shard_map/all_to_all | solution.py:183
  95.9 0.3 copy.46
  96.2 0.9 reshape.24.alpha_ref
  97.1 0.0 all-gather.3.cloned.1.call-done
  97.1 46.7 %sigma_block.1 = bf16[64,1536]{1,0:T(8,128)(2,1)} custom-call(s32[1536,32]{1,0:T(8,128)} %fusion.3.idx_ref, f32[1536,64]{1,0:T(8,128)} %maximum_bitcast_fusion.w_ref, f32[64,1536]{1,0:T(8,128)} %reshape.24.alpha_ref, bf16[4,8,1536,128]{3,2,1,0:T(8,128)(2,1)} %bitcast.27), custom_call_target="tpu_custom_call" | custom-call | flops 6448742400 | bytes 13565952 | tf_op jit(solution)/shard_map/sigma_block/pallas_call | solution.py:130
  143.8 1.1 pad_maximum_fusion
  144.8 39.3 %all_to_all.15 = bf16[8,16,1536]{2,1,0:T(8,128)(2,1)S(1)} all-to-all(bf16[8,16,1536]{2,1,0:T(8,128)(2,1)S(1)} %pad_maximum_fusion), channel_id=1, replica_groups={{0,128,256,384,1,129,257,385},{16,144,272,400,17,145,273,401},{32,160,2..., dimensions={0} | all-to-all | bytes 786432 | tf_op jit(solution)/shard_map/all_to_all | solution.py:207
  184.2 0.8 copy.48
  (2 shorter events, 0.0 us)
Async XLA Ops:
  6.5 50.4 %copy-start = (bf16[512,512]{1,0:T(8,128)(2,1)S(1)}, bf16[512,512]{1,0:T(8,128)(2,1)}, u32[]{:S(2)}) copy-start(bf16[512,512]{1,0:T(8,128)(2,1)} %param.5) | copy-start | bytes 1572868
  6.5 90.6 %all-gather.3.cloned.1.call-start = ((), (), s32[]{:S(2)}) async-start(), calls=%async_computation.3 | async-start | bytes 12976128 | tf_op jit(solution)/shard_map/all_gather | solution.py:174
  10.7 46.3 %all-to-all-start = ((bf16[32,16,192]{2,1,0:T(8,128)(2,1)}), bf16[32,16,192]{2,1,0:T(8,128)(2,1)S(1)}, u32[]{:S(2)}, u32[]{:S(2)}) async-start(bf16[32,16,192]{2,1,0:T(8,128)(2,1)} %copy.43), calls=%async_computation | async-start | bytes 524288 | tf_op jit(solution)/shard_map/all_to_all | solution.py:180
  27.1 16.4 %collective-permute-start.1 = (f32[16,1536]{1,0:T(8,128)S(1)}, f32[16,1536]{1,0:T(8,128)S(1)}, u32[]{:S(2)}, u32[]{:S(2)}) collective-permute-start(f32[16,1536]{1,0:T(8,128)S(1)} %get-tuple-element.8), channel_id=1, source_target_pairs={{0,1},{1,0},{2,3},{3,2},{4,5},{5,4},{6,7},{7,6},{8,9},{9,8},{10,11... | collective-permute-start | bytes 294920 | tf_op jit(solution)/shard_map/ppermute | solution.py:190
  36.3 20.4 %collective-permute-start = (s32[16,1536]{1,0:T(8,128)S(1)}, s32[16,1536]{1,0:T(8,128)S(1)}, u32[]{:S(2)}, u32[]{:S(2)}) collective-permute-start(s32[16,1536]{1,0:T(8,128)S(1)} %get-tuple-element.10), channel_id=1, source_target_pairs={{0,1},{1,0},{2,3},{3,2},{4,5},{5,4},{6,7},{7,6},{8,9},{9,8},{10,11... | collective-permute-start | bytes 294920 | tf_op jit(solution)/shard_map/ppermute | solution.py:190
  58.3 37.5 %all-to-all-start.1 = ((f32[8,4,16,192]{3,2,1,0:T(8,128)}), f32[8,4,16,192]{3,2,1,0:T(8,128)S(1)}, u32[]{:S(2)}, u32[]{:S(2)}) async-start(f32[8,4,16,192]{3,2,1,0:T(8,128)} %copy.45), calls=%async_computation.1 | async-start | bytes 1048576 | tf_op jit(solution)/shard_map/all_to_all | solution.py:183
Sparse Core Ops, SparseCore 0:
  10.5 82.2 all-gather.2

commit v4 on v3

v4 whole, which is shorter than its diff:
```python
import functools

import jax
import jax.numpy as jnp
from jax import lax
from jax.experimental import pallas as pl
from jax.experimental.pallas import tpu as pltpu
from jax.sharding import PartitionSpec as P

Y = 4
Z = 8
LANES = 128


def pack_kernel(turn_ref, in_ref, out_ref):
    alphas, betas = in_ref.shape
    groups = LANES // alphas
    rows = betas // groups
    for c in range(rows // LANES):
        parts = []
        for block in range(groups):
            group = lax.rem(block + groups - turn_ref[0], groups)
            start = pl.multiple_of(group * rows + c * LANES, LANES)
            parts.append(in_ref[:, pl.ds(start, LANES)])
        tile = jnp.concatenate(parts, axis=0).astype(jnp.float32)
        out_ref[pl.ds(c * LANES, LANES), :] = tile.T.astype(out_ref.dtype)


def pack_rows(coeffs, turn):
    alphas, betas = coeffs.shape
    return pl.pallas_call(
        pack_kernel,
        in_specs=[
            pl.BlockSpec(memory_space=pltpu.SMEM),
            pl.BlockSpec(memory_space=pltpu.VMEM),
        ],
        out_specs=pl.BlockSpec(memory_space=pltpu.VMEM),
        out_shape=jax.ShapeDtypeStruct((alphas * betas // LANES, LANES), coeffs.dtype),
        name="pack_rows",
    )(turn.reshape(1), coeffs)


def beta_kernel(
    chunk,
    idx_ref, w_ref, own_ref, other_ref, out_ref,
    table, stage, spread, acc_ref, near, sems, near_sems,
):
    _, classes, rows, _ = own_ref.shape
    per_class = rows // chunk
    chunks = classes * per_class
    depth = stage.shape[0]
    buffers, batch, slots = near.shape
    targets = w_ref.shape[0]
    rounds = targets // (buffers * batch)

    def fetch(packed_ref, c, slot):
        start = pl.multiple_of(lax.rem(c, per_class) * chunk, 16)
        return pltpu.make_async_copy(
            packed_ref.at[:, c // per_class, pl.ds(start, chunk), :], stage.at[slot], sems.at[slot]
        )

    def bring(r, b):
        start = pl.multiple_of((r * buffers + b) * batch, batch)
        return pltpu.make_async_copy(
            idx_ref.at[pl.ds(start, batch), :], near.at[b], near_sems.at[b]
        )

    for c in range(depth - 1):
        fetch(own_ref, c, c).start()
    for b in range(buffers):
        bring(0, b).start()

    size = 2 * LANES
    source = lax.broadcasted_iota(jnp.int32, (size, size), 0)
    column = lax.broadcasted_iota(jnp.int32, (size, size), 1)
    for m in range(Y // 2):
        turn = 2 * m + (column >> 7)
        wanted = (column & 128) + ((column + 16 * turn) & 127)
        spread[m] = jnp.where(source == wanted, 1.0, 0.0).astype(spread.dtype)
    piece = 256
    lane_part = (lax.broadcasted_iota(jnp.int32, (piece, LANES), 1) >> 4) & 3

    @pl.loop(0, 2 * chunks)
    def _(c):
        slot = lax.rem(c, depth)
        ahead = c + depth - 1

        @pl.when(ahead < chunks)
        def _():
            fetch(own_ref, ahead, lax.rem(ahead, depth)).start()

        @pl.when(jnp.logical_and(ahead >= chunks, ahead < 2 * chunks))
        def _():
            fetch(other_ref, ahead - chunks, lax.rem(ahead, depth)).start()

        fetch(own_ref, lax.rem(c, chunks), slot).wait()
        first = (c // per_class) * (Y * rows) + lax.rem(c, per_class) * chunk
        for at in range(0, chunk, piece):
            shards = [stage[slot, y, pl.ds(at, piece), :] for y in range(Y)]
            mixed = []
            for g in range(Y):
                rows_g = shards[(Y - 1 - g) % Y]
                for j in range(Y - 1):
                    rows_g = jnp.where(lane_part == j, shards[(j - g) % Y], rows_g)
                mixed.append(rows_g)
            for m in range(Y // 2):
                turned = jnp.dot(
                    jnp.concatenate(mixed[2 * m : 2 * m + 2], axis=1),
                    spread[m],
                    preferred_element_type=jnp.float32,
                )
                for g in (2 * m, 2 * m + 1):
                    to = pl.multiple_of(first + (g * rows + at), 8)
                    lanes = (g - 2 * m) * LANES
                    table[pl.ds(to, piece), :] = turned[:, lanes : lanes + LANES]

    lane_row = lax.broadcasted_iota(jnp.int32, (8, LANES), 0)
    low_lane = lax.broadcasted_iota(jnp.int32, (8, LANES), 1) < LANES // 2

    @pl.loop(0, rounds)
    def _(r):
        for b in range(buffers):
            bring(r, b).wait()
            for g in range(0, batch, 8):
                base = pl.multiple_of((r * buffers + b) * batch + g, 8)
                weights = w_ref[pl.ds(base, 8), :]
                total = jnp.zeros((8, LANES), jnp.float32)
                for q in range(slots):
                    picked = None
                    for k in range(8):
                        row = table[pl.ds(near[b, g + k, q], 1), :]
                        row = jnp.broadcast_to(row, (8, LANES))
                        picked = row if k == 0 else jnp.where(lane_row == k, row, picked)
                    low = jnp.broadcast_to(weights[:, q : q + 1], (8, LANES))
                    high = jnp.broadcast_to(weights[:, slots + q : slots + q + 1], (8, LANES))
                    total = total + picked * jnp.where(low_lane, low, high)
                acc_ref[pl.ds(base, 8), :] = total

            @pl.when(r + 1 < rounds)
            def _():
                bring(r + 1, b).start()

    alphas = out_ref.shape[0]
    for at in range(0, targets, LANES):
        turned = acc_ref[pl.ds(at, LANES), :].T
        out_ref[:, pl.ds(at, LANES)] = turned[:alphas, :] + turned[alphas:, :]


def beta_block(idx, weights, own, other, chunk=768, depth=4, buffers=2, batch=32):
    targets, slots = idx.shape
    _, classes, rows, _ = own.shape
    pairs = 2 * classes * rows * Y
    alphas = LANES // 2
    return pl.pallas_call(
        functools.partial(beta_kernel, chunk),
        in_specs=[
            pl.BlockSpec(memory_space=pl.ANY),
            pl.BlockSpec(memory_space=pltpu.VMEM),
            pl.BlockSpec(memory_space=pl.ANY),
            pl.BlockSpec(memory_space=pl.ANY),
        ],
        out_specs=pl.BlockSpec(memory_space=pltpu.VMEM),
        out_shape=jax.ShapeDtypeStruct((alphas, targets), jnp.float32),
        scratch_shapes=[
            pltpu.VMEM((pairs, LANES), jnp.float32),
            pltpu.VMEM((depth, Y, chunk, LANES), jnp.bfloat16),
            pltpu.VMEM((Y // 2, 2 * LANES, 2 * LANES), jnp.bfloat16),
            pltpu.VMEM((targets, LANES), jnp.float32),
            pltpu.SMEM((buffers, batch, slots), jnp.int32),
            pltpu.SemaphoreType.DMA((depth,)),
            pltpu.SemaphoreType.DMA((buffers,)),
        ],
        compiler_params=pltpu.CompilerParams(vmem_limit_bytes=36 * 2**20),
        cost_estimate=pl.CostEstimate(
            flops=2 * pairs * LANES * Y * LANES,
            bytes_accessed=pairs * LANES * 2 + targets * slots * 8 + alphas * targets * 4,
            transcendentals=0,
        ),
        name="beta_block",
    )(idx, weights, own, other)


def per_device(coeffs, alpha_coupling, parent_string_index, excitation_weight):
    own_rows, betas = coeffs.shape
    strings = alpha_coupling.shape[0]
    reps = lax.axis_size("rep")
    cols = lax.axis_size("col")
    parts = reps * Y
    part = betas // parts
    small = part // Z
    along_z = [[y * Z + z for z in range(Z)] for y in range(Y)]
    y_and_x = [
        [(y * Z + z) * cols + 2 * x + core for y in range(Y) for x in range(cols // 2)]
        for z in range(Z)
        for core in range(2)
    ]
    row = lax.axis_index("row")
    rep = lax.axis_index("rep")
    core = lax.axis_index("col") % 2
    mine = (rep * Y + row // Z) * part
    theirs = ((1 - rep) * Y + row // Z) * part

    own = lax.all_gather(
        pack_rows(coeffs, row // Z), ("row", "col"), axis=0, axis_index_groups=y_and_x
    ).reshape(Y, cols // 2, -1, LANES)

    half = lax.dynamic_slice_in_dim(coeffs, rep * (Y * part), Y * part, 1)
    pieces = half.reshape(own_rows, Y * Z, small).transpose(1, 0, 2)
    columns = lax.all_to_all(pieces, "row", 0, 0).reshape(strings, small)
    alpha_term = jnp.dot(alpha_coupling, columns, preferred_element_type=jnp.float32)
    alpha_term = alpha_term.reshape(Y, Z, own_rows, small).transpose(1, 0, 2, 3)

    sent = jnp.concatenate(
        [
            lax.dynamic_slice_in_dim(parent_string_index, theirs, part, 1).astype(jnp.float32),
            lax.dynamic_slice_in_dim(excitation_weight, theirs, part, 1),
        ],
        axis=0,
    )
    got = lax.ppermute(sent, "rep", [(0, 1), (1, 0)])
    slots = parent_string_index.shape[0]
    idx = jnp.concatenate(
        [
            lax.dynamic_slice_in_dim(parent_string_index, mine, part, 1),
            got[:slots].astype(jnp.int32),
        ],
        axis=0,
    )
    weights = jnp.concatenate(
        [lax.dynamic_slice_in_dim(excitation_weight, mine, part, 1), got[slots:]], axis=0
    )
    halves = idx // (betas // 2)
    place = (((halves >> 1) & 1) ^ core) * (cols // 2) + (halves >> 2)
    upper = (halves & 1) == 1
    idx = (idx + (place - halves) * (betas // 2)).T
    weights = jnp.concatenate(
        [jnp.where(upper, 0.0, weights), jnp.where(upper, weights, 0.0)], axis=0
    ).T

    own, idx, weights, alpha_term = lax.optimization_barrier((own, idx, weights, alpha_term))
    other = lax.ppermute(own, "col", [(c, c ^ 1) for c in range(cols)])
    alpha_term = lax.all_to_all(alpha_term, "row", 0, 0, axis_index_groups=along_z)
    alpha_term = alpha_term.transpose(1, 2, 0, 3).reshape(Y * own_rows, part)

    beta_term = beta_block(idx, weights, own, other)
    sigma = (alpha_term + beta_term).astype(jnp.bfloat16)
    pieces = sigma.reshape(Y, own_rows, part)
    pieces = jnp.concatenate([pieces, pieces], axis=0)
    back = [[r * Y * Z + y * Z + z for r in range(reps) for y in range(Y)] for z in range(Z)]
    done = lax.all_to_all(pieces, ("rep", "row"), 0, 0, axis_index_groups=back, tiled=True)
    return done.reshape(parts, own_rows, part).transpose(1, 0, 2).reshape(own_rows, betas)


def solution(mesh):
    placed = (P("row", "col"), P(), P("rep", "col"), P("rep", "col"))
    return jax.shard_map(
        per_device, mesh=mesh, in_specs=placed, out_specs=P("row", "col"), check_vma=False
    )
```

time: 192 us -> 221 us (1.15)
  blocking collectives: 39.3 us -> 73 us
  waiting for transfers between devices: 35.6 us -> 52.5 us
  starting transfers between devices: 41.5 us -> 25.5 us
  Pallas kernels: 48.7 us -> 44.9 us
  other arithmetic: 5.22 us -> 2.72 us
    all_to_all x0 -> x1, blocking collectives: none -> 37.8 us  [per_device(): lax.all_to_all(alpha_term, 'row', 0, 0, axis_index_groups=along_z)]
    all_gather x1, waiting for transfers between devices: 0.01 us -> 34.2 us  [per_device(): lax.all_gather(pack_rows(coeffs, row // Z), ('row', 'col'), axis=0, axis_...]
    all_to_all x1 -> x0, waiting for transfers between devices: 21.9 us -> none  [per_device(): lax.all_to_all(alpha_term, 'row', 0, 0, axis_index_groups=along_z)]
    all_to_all x1, waiting for transfers between devices: 0.01 us -> 11.8 us  [per_device(): columns = lax.all_to_all(pieces, 'row', 0, 0).reshape(strings, small)]
    all_to_all x1 -> x0, starting transfers between devices: 11.5 us -> none  [per_device(): lax.all_to_all(alpha_term, 'row', 0, 0, axis_index_groups=along_z)]
    ppermute x2, waiting for transfers between devices: 13.7 us -> 6.44 us  [the longest x1 6.44 us: per_device(): got = lax.ppermute(sent, 'rep', [(0, 1), (1, 0)])]
    all_to_all x1, starting transfers between devices: 15.4 us -> 8.81 us  [per_device(): columns = lax.all_to_all(pieces, 'row', 0, 0).reshape(strings, small)]
    all_to_all x1, blocking collectives: 39.3 us -> 35.2 us  [per_device(): lax.all_to_all(pieces, ('rep', 'row'), 0, 0, axis_index_groups=back, tile...]
  transfers between devices with their start and end apart: 5 -> 4, of which waited for: 3 -> 3; matrix products, arithmetic and copies ran while one was open for 6% -> 3% of each run, Pallas kernels for 0% -> 0%
where the time goes in v4:
time: 221 us; the launch traced here: 220 us
  blocking collectives  73 us (33%)
  waiting for transfers between devices  52.5 us (24%)
  Pallas kernels  44.9 us (20%)
  starting transfers between devices  25.5 us (12%)
  between operations  13.6 us (6%)
  local copies, waits for them, and re-layouts  7.87 us (4%)
  other arithmetic  2.72 us (1%)
    pallas_call x1, Pallas kernels, beta_block(): pl.pallas_call(functools.partial(beta_kernel, chunk), in_specs=[pl.BlockS...  42.9 us
    all_to_all x1, blocking collectives, per_device(): lax.all_to_all(alpha_term, 'row', 0, 0, axis_index_groups=along_z)  37.8 us
    all_to_all x1, blocking collectives, per_device(): lax.all_to_all(pieces, ('rep', 'row'), 0, 0, axis_index_groups=back, tile...  35.2 us
    all_gather x1, waiting for transfers between devices, per_device(): lax.all_gather(pack_rows(coeffs, row // Z), ('row', 'col'), axis=0, axis_...  34.2 us
    ppermute x1, starting transfers between devices, per_device(): got = lax.ppermute(sent, 'rep', [(0, 1), (1, 0)])  14.8 us
    all_to_all x1, waiting for transfers between devices, per_device(): columns = lax.all_to_all(pieces, 'row', 0, 0).reshape(strings, small)  11.8 us
    all_to_all x1, starting transfers between devices, per_device(): columns = lax.all_to_all(pieces, 'row', 0, 0).reshape(strings, small)  8.81 us
    ppermute x1, waiting for transfers between devices, per_device(): got = lax.ppermute(sent, 'rep', [(0, 1), (1, 0)])  6.44 us
  transfers between devices with their start and end apart: 4, of which 3 were waited for; matrix products, arithmetic and copies ran while one was open for 3% of the time, Pallas kernels for 0%

profile of v4, /device:TPU:32, one launch (start us, length us, event | category | flops | bytes accessed | tf_op | source)
XLA Modules:
  0.0 220.5 jit_solution(13332284551291606428)
XLA Ops:
  6.5 0.0 copy-start
  6.5 0.0 all-gather.3.cloned.1.call-start
  6.5 2.0 pack_rows.1
  8.5 0.0 all-gather.3.cloned.1.call-update
  8.6 1.0 constant_dynamic-slice_fusion.3
  9.5 1.0 constant_dynamic-slice_fusion.1
  10.5 14.8 %collective-permute-start = (f32[32,1536]{1,0:T(8,128)S(1)}, f32[32,1536]{1,0:T(8,128)S(1)}, u32[]{:S(2)}, u32[]{:S(2)}) collective-permute-start(f32[32,1536]{1,0:T(8,128)S(1)} %pad_maximum_fusion.1), channel_id=1, source_target_pairs={{0,1},{1,0},{2,3},{3,2},{4,5},{5,4},{6,7},{7,6},{8,9},{9,8},{10,11... | collective-permute-start | bytes 589832 | tf_op jit(solution)/shard_map/ppermute | solution.py:220
  25.4 0.9 constant_dynamic-slice_fusion
  26.3 0.3 reshape.26
  26.6 0.9 copy.43
  27.5 8.8 %all-to-all-start = ((bf16[32,16,192]{2,1,0:T(8,128)(2,1)}), bf16[32,16,192]{2,1,0:T(8,128)(2,1)S(1)}, u32[]{:S(2)}, u32[]{:S(2)}) async-start(bf16[32,16,192]{2,1,0:T(8,128)(2,1)} %copy.43), calls=%async_computation | async-start | bytes 524288 | tf_op jit(solution)/shard_map/all_to_all | solution.py:209
  36.3 6.4 %collective-permute-done = f32[32,1536]{1,0:T(8,128)S(1)} collective-permute-done((f32[32,1536]{1,0:T(8,128)S(1)}, f32[32,1536]{1,0:T(8,128)S(1)}, u32[]{:S(2)}, u32[]{:S(2)}) %collective-permute-start) | collective-permute-done | bytes 196640 | tf_op jit(solution)/shard_map/ppermute | solution.py:220
  42.8 0.3 copy.40
  43.1 0.3 copy.41
  43.4 0.6 broadcast_select_fusion.1
  44.0 0.3 maximum_bitcast_fusion.w_ref
  44.3 0.7 add_bitcast_fusion.idx_ref
  45.0 11.8 %all-to-all-done = bf16[32,16,192]{2,1,0:T(8,128)(2,1)S(1)} async-done(((bf16[32,16,192]{2,1,0:T(8,128)(2,1)}), bf16[32,16,192]{2,1,0:T(8,128)(2,1)S(1)}, u32[]{:S(2)}, u32[]{:S(2)}) %all-to-all-start) | async-done | bytes 196640 | tf_op jit(solution)/shard_map/all_to_all | solution.py:209
  56.8 0.0 copy-done
  56.8 0.3 convolution_bitcast_fusion
  57.2 0.2 copy.44
  57.4 34.2 %all-gather.3.cloned.1.call-done = bf16[24576,128]{1,0:T(8,128)(2,1)} async-done(((bf16[1536,128]{1,0:T(8,128)(2,1)}), bf16[24576,128]{1,0:T(8,128)(2,1)}) %all-gather.3.cloned.1.call-update) | async-done | bytes 6291472 | tf_op jit(solution)/shard_map/all_gather | solution.py:203
  91.6 1.9 collective-permute-start.1
  93.5 37.8 %all_to_all.15 = f32[8,4,16,192]{3,2,1,0:T(8,128)S(1)} all-to-all(f32[8,4,16,192]{3,2,1,0:T(8,128)S(1)} %copy.45), channel_id=1, replica_groups={{0,16,32,48,64,80,96,112},{128,144,160,176,192,208,224,240},{256,272,28..., dimensions={0} | all-to-all | bytes 786432 | tf_op jit(solution)/shard_map/all_to_all | solution.py:242
  131.4 0.3 copy.46
  131.7 0.2 reshape.29
  131.9 0.0 collective-permute-done.1.other_ref
  131.9 0.0 copy-start.1
  131.9 2.8 %copy-done.1 = bf16[24576,128]{1,0:T(8,128)(2,1)S(1)} copy-done((bf16[24576,128]{1,0:T(8,128)(2,1)S(1)}, bf16[24576,128]{1,0:T(8,128)(2,1)}, u32[]{:S(2)}) %copy-start.1) | copy-done | bytes 6291480
  134.7 42.9 %beta_block.1 = f32[64,1536]{1,0:T(8,128)S(1)} custom-call(s32[1536,32]{1,0:T(8,128)S(1)} %add_bitcast_fusion.idx_ref, f32[1536,64]{1,0:T(8,128)S(1)} %maximum_bitcast_fusion.w_ref, bf16[4,4,1536,128]{3,2,1,0:T(8,128)(2,1)S(1)} %bitcast.23, bf16[4,4,1536,128]{3,2,1,0:T(8,128)(2,1)} %collective-permute-done.1.other_ref), custom_call_target="tpu_custom_call" | custom-call | flops 6442450944 | bytes 13369344 | tf_op jit(solution)/shard_map/beta_block/pallas_call | solution.py:154
  177.6 35.2 %all_to_all.16 = bf16[8,16,1536]{2,1,0:T(8,128)(2,1)S(1)} all-to-all(bf16[8,16,1536]{2,1,0:T(8,128)(2,1)S(1)} %pad_maximum_fusion), channel_id=1, replica_groups={{0,128,256,384,1,129,257,385},{16,144,272,400,17,145,273,401},{32,160,2..., dimensions={0} | all-to-all | bytes 786432 | tf_op jit(solution)/shard_map/all_to_all | solution.py:250
  212.8 0.8 copy.48
  (7 shorter events, 0.2 us)
Async XLA Ops:
  6.5 50.3 %copy-start = (bf16[512,512]{1,0:T(8,128)(2,1)S(1)}, bf16[512,512]{1,0:T(8,128)(2,1)}, u32[]{:S(2)}) copy-start(bf16[512,512]{1,0:T(8,128)(2,1)} %param.5) | copy-start | bytes 1572868
  6.5 85.0 %all-gather.3.cloned.1.call-start = ((), (), s32[]{:S(2)}) async-start(), calls=%async_computation.3 | async-start | bytes 6684672 | tf_op jit(solution)/shard_map/all_gather | solution.py:203
  10.5 32.2 %collective-permute-start = (f32[32,1536]{1,0:T(8,128)S(1)}, f32[32,1536]{1,0:T(8,128)S(1)}, u32[]{:S(2)}, u32[]{:S(2)}) collective-permute-start(f32[32,1536]{1,0:T(8,128)S(1)} %pad_maximum_fusion.1), channel_id=1, source_target_pairs={{0,1},{1,0},{2,3},{3,2},{4,5},{5,4},{6,7},{7,6},{8,9},{9,8},{10,11... | collective-permute-start | bytes 589832 | tf_op jit(solution)/shard_map/ppermute | solution.py:220
  27.5 29.3 %all-to-all-start = ((bf16[32,16,192]{2,1,0:T(8,128)(2,1)}), bf16[32,16,192]{2,1,0:T(8,128)(2,1)S(1)}, u32[]{:S(2)}, u32[]{:S(2)}) async-start(bf16[32,16,192]{2,1,0:T(8,128)(2,1)} %copy.43), calls=%async_computation | async-start | bytes 524288 | tf_op jit(solution)/shard_map/all_to_all | solution.py:209
  91.6 40.3 %collective-permute-start.1 = (bf16[4,4,1536,128]{3,2,1,0:T(8,128)(2,1)}, bf16[4,4,1536,128]{3,2,1,0:T(8,128)(2,1)}, u32[]{:S(2)}, u32[]{:S(2)}) collective-permute-start(bf16[4,4,1536,128]{3,2,1,0:T(8,128)(2,1)} %bitcast.22), channel_id=1, source_target_pairs={{0,2},{2,0},{4,6},{6,4},{8,10},{10,8},{12,14},{14,12},{1,3},{3,1},... | collective-permute-start | bytes 18874376 | tf_op jit(solution)/shard_map/ppermute | solution.py:241
  131.9 2.8 %copy-start.1 = (bf16[24576,128]{1,0:T(8,128)(2,1)S(1)}, bf16[24576,128]{1,0:T(8,128)(2,1)}, u32[]{:S(2)}) copy-start(bf16[24576,128]{1,0:T(8,128)(2,1)} %all-gather.3.cloned.1.call-done) | copy-start | bytes 18874372
Sparse Core Ops, SparseCore 0:
  10.4 81.1 all-gather.2

commit v5 on v4

--- a/solution.py
+++ b/solution.py
@@ -40,35 +40,22 @@
     )(turn.reshape(1), coeffs)
 
 
-def beta_kernel(
-    chunk,
-    idx_ref, w_ref, own_ref, other_ref, out_ref,
-    table, stage, spread, acc_ref, near, sems, near_sems,
-):
-    _, classes, rows, _ = own_ref.shape
+def table_kernel(chunk, packed_ref, table, stage, spread, sems):
+    _, classes, rows, _ = packed_ref.shape
     per_class = rows // chunk
     chunks = classes * per_class
     depth = stage.shape[0]
-    buffers, batch, slots = near.shape
-    targets = w_ref.shape[0]
-    rounds = targets // (buffers * batch)
-
-    def fetch(packed_ref, c, slot):
+
+    def fetch(c, slot):
         start = pl.multiple_of(lax.rem(c, per_class) * chunk, 16)
         return pltpu.make_async_copy(
-            packed_ref.at[:, c // per_class, pl.ds(start, chunk), :], stage.at[slot], sems.at[slot]
+            packed_ref.at[:, lax.div(c, per_class), pl.ds(start, chunk), :],
+            stage.at[slot],
+            sems.at[slot],
         )
 
-    def bring(r, b):
-        start = pl.multiple_of((r * buffers + b) * batch, batch)
-        return pltpu.make_async_copy(
-            idx_ref.at[pl.ds(start, batch), :], near.at[b], near_sems.at[b]
-        )
-
     for c in range(depth - 1):
-        fetch(own_ref, c, c).start()
-    for b in range(buffers):
-        bring(0, b).start()
+        fetch(c, c).start()
 
     size = 2 * LANES
     source = lax.broadcasted_iota(jnp.int32, (size, size), 0)
@@ -80,21 +67,16 @@
     piece = 256
     lane_part = (lax.broadcasted_iota(jnp.int32, (piece, LANES), 1) >> 4) & 3
 
-    @pl.loop(0, 2 * chunks)
+    @pl.loop(0, chunks)
     def _(c):
         slot = lax.rem(c, depth)
-        ahead = c + depth - 1
-
-        @pl.when(ahead < chunks)
+
+        @pl.when(c + depth - 1 < chunks)
         def _():
-            fetch(own_ref, ahead, lax.rem(ahead, depth)).start()
-
-        @pl.when(jnp.logical_and(ahead >= chunks, ahead < 2 * chunks))
-        def _():
-            fetch(other_ref, ahead - chunks, lax.rem(ahead, depth)).start()
-
-        fetch(own_ref, lax.rem(c, chunks), slot).wait()
-        first = (c // per_class) * (Y * rows) + lax.rem(c, per_class) * chunk
+            fetch(c + depth - 1, lax.rem(c + depth - 1, depth)).start()
+
+        fetch(c, slot).wait()
+        first = lax.div(c, per_class) * (Y * rows) + lax.rem(c, per_class) * chunk
         for at in range(0, chunk, piece):
             shards = [stage[slot, y, pl.ds(at, piece), :] for y in range(Y)]
             mixed = []
@@ -114,6 +96,42 @@
                     lanes = (g - 2 * m) * LANES
                     table[pl.ds(to, piece), :] = turned[:, lanes : lanes + LANES]
 
+
+def build_table(packed, chunk=768, depth=4):
+    _, classes, rows, _ = packed.shape
+    pairs = classes * rows * Y
+    return pl.pallas_call(
+        functools.partial(table_kernel, chunk),
+        in_specs=[pl.BlockSpec(memory_space=pl.ANY)],
+        out_specs=pl.BlockSpec(memory_space=pltpu.VMEM),
+        out_shape=pltpu.VMEM((pairs, LANES), jnp.float32),
+        scratch_shapes=[
+            pltpu.VMEM((depth, Y, chunk, LANES), jnp.bfloat16),
+            pltpu.VMEM((Y // 2, 2 * LANES, 2 * LANES), jnp.bfloat16),
+            pltpu.SemaphoreType.DMA((depth,)),
+        ],
+        compiler_params=pltpu.CompilerParams(vmem_limit_bytes=30 * 2**20),
+        cost_estimate=pl.CostEstimate(
+            flops=2 * pairs * LANES * Y * LANES, bytes_accessed=packed.size * 2, transcendentals=0
+        ),
+        name="build_table",
+    )(packed)
+
+
+def pick_kernel(table, idx_ref, w_ref, alpha_ref, out_ref, acc_ref, near, near_sems):
+    buffers, batch, slots = near.shape
+    targets = w_ref.shape[0]
+    rounds = targets // (buffers * batch)
+
+    def bring(r, b):
+        start = pl.multiple_of((r * buffers + b) * batch, batch)
+        return pltpu.make_async_copy(
+            idx_ref.at[pl.ds(start, batch), :], near.at[b], near_sems.at[b]
+        )
+
+    for b in range(buffers):
+        bring(0, b).start()
+
     lane_row = lax.broadcasted_iota(jnp.int32, (8, LANES), 0)
     low_lane = lax.broadcasted_iota(jnp.int32, (8, LANES), 1) < LANES // 2
 
@@ -143,41 +161,38 @@
     alphas = out_ref.shape[0]
     for at in range(0, targets, LANES):
         turned = acc_ref[pl.ds(at, LANES), :].T
-        out_ref[:, pl.ds(at, LANES)] = turned[:alphas, :] + turned[alphas:, :]
-
-
-def beta_block(idx, weights, own, other, chunk=768, depth=4, buffers=2, batch=32):
+        beta_term = turned[:alphas, :] + turned[alphas:, :]
+        total = alpha_ref[:, pl.ds(at, LANES)] + beta_term
+        out_ref[:, pl.ds(at, LANES)] = total.astype(out_ref.dtype)
+
+
+def sigma_block(table, idx, weights, alpha_term, buffers=2, batch=32):
     targets, slots = idx.shape
-    _, classes, rows, _ = own.shape
-    pairs = 2 * classes * rows * Y
-    alphas = LANES // 2
+    alphas = alpha_term.shape[0]
+    table = pltpu.with_memory_space_constraint(table, pltpu.VMEM)
     return pl.pallas_call(
-        functools.partial(beta_kernel, chunk),
+        pick_kernel,
         in_specs=[
+            pl.BlockSpec(memory_space=pltpu.VMEM),
             pl.BlockSpec(memory_space=pl.ANY),
             pl.BlockSpec(memory_space=pltpu.VMEM),
-            pl.BlockSpec(memory_space=pl.ANY),
-            pl.BlockSpec(memory_space=pl.ANY),
+            pl.BlockSpec(memory_space=pltpu.VMEM),
         ],
         out_specs=pl.BlockSpec(memory_space=pltpu.VMEM),
-        out_shape=jax.ShapeDtypeStruct((alphas, targets), jnp.float32),
+        out_shape=jax.ShapeDtypeStruct((alphas, targets), jnp.bfloat16),
         scratch_shapes=[
-            pltpu.VMEM((pairs, LANES), jnp.float32),
-            pltpu.VMEM((depth, Y, chunk, LANES), jnp.bfloat16),
-            pltpu.VMEM((Y // 2, 2 * LANES, 2 * LANES), jnp.bfloat16),
             pltpu.VMEM((targets, LANES), jnp.float32),
             pltpu.SMEM((buffers, batch, slots), jnp.int32),
-            pltpu.SemaphoreType.DMA((depth,)),
             pltpu.SemaphoreType.DMA((buffers,)),
         ],
-        compiler_params=pltpu.CompilerParams(vmem_limit_bytes=36 * 2**20),
+        compiler_params=pltpu.CompilerParams(vmem_limit_bytes=30 * 2**20),
         cost_estimate=pl.CostEstimate(
-            flops=2 * pairs * LANES * Y * LANES,
-            bytes_accessed=pairs * LANES * 2 + targets * slots * 8 + alphas * targets * 4,
+            flops=40 * targets * slots * LANES,
+            bytes_accessed=40 * targets * slots * LANES,
             transcendentals=0,
         ),
-        name="beta_block",
-    )(idx, weights, own, other)
+        name="sigma_block",
+    )(table, idx, weights, alpha_term)
 
 
 def per_device(coeffs, alpha_coupling, parent_string_index, excitation_weight):
@@ -189,26 +204,23 @@
     part = betas // parts
     small = part // Z
     along_z = [[y * Z + z for z in range(Z)] for y in range(Y)]
-    y_and_x = [
-        [(y * Z + z) * cols + 2 * x + core for y in range(Y) for x in range(cols // 2)]
-        for z in range(Z)
-        for core in range(2)
-    ]
+    y_and_col = [[(y * Z + z) * cols + c for y in range(Y) for c in range(cols)] for z in range(Z)]
     row = lax.axis_index("row")
     rep = lax.axis_index("rep")
-    core = lax.axis_index("col") % 2
     mine = (rep * Y + row // Z) * part
     theirs = ((1 - rep) * Y + row // Z) * part
 
-    own = lax.all_gather(
-        pack_rows(coeffs, row // Z), ("row", "col"), axis=0, axis_index_groups=y_and_x
-    ).reshape(Y, cols // 2, -1, LANES)
+    packed = lax.all_gather(
+        pack_rows(coeffs, row // Z), ("row", "col"), axis=0, axis_index_groups=y_and_col
+    ).reshape(Y, cols, -1, LANES)
 
     half = lax.dynamic_slice_in_dim(coeffs, rep * (Y * part), Y * part, 1)
     pieces = half.reshape(own_rows, Y * Z, small).transpose(1, 0, 2)
     columns = lax.all_to_all(pieces, "row", 0, 0).reshape(strings, small)
     alpha_term = jnp.dot(alpha_coupling, columns, preferred_element_type=jnp.float32)
     alpha_term = alpha_term.reshape(Y, Z, own_rows, small).transpose(1, 0, 2, 3)
+    alpha_term = lax.all_to_all(alpha_term, "row", 0, 0, axis_index_groups=along_z)
+    alpha_term = alpha_term.transpose(1, 2, 0, 3).reshape(Y * own_rows, part)
 
     sent = jnp.concatenate(
         [
@@ -230,24 +242,28 @@
         [lax.dynamic_slice_in_dim(excitation_weight, mine, part, 1), got[slots:]], axis=0
     )
     halves = idx // (betas // 2)
-    place = (((halves >> 1) & 1) ^ core) * (cols // 2) + (halves >> 2)
     upper = (halves & 1) == 1
-    idx = (idx + (place - halves) * (betas // 2)).T
+    idx = (idx - ((halves + 1) >> 1) * (betas // 2)).T
     weights = jnp.concatenate(
         [jnp.where(upper, 0.0, weights), jnp.where(upper, weights, 0.0)], axis=0
     ).T
 
-    own, idx, weights, alpha_term = lax.optimization_barrier((own, idx, weights, alpha_term))
-    other = lax.ppermute(own, "col", [(c, c ^ 1) for c in range(cols)])
-    alpha_term = lax.all_to_all(alpha_term, "row", 0, 0, axis_index_groups=along_z)
-    alpha_term = alpha_term.transpose(1, 2, 0, 3).reshape(Y * own_rows, part)
-
-    beta_term = beta_block(idx, weights, own, other)
-    sigma = (alpha_term + beta_term).astype(jnp.bfloat16)
-    pieces = sigma.reshape(Y, own_rows, part)
-    pieces = jnp.concatenate([pieces, pieces], axis=0)
+    table = build_table(packed)
     back = [[r * Y * Z + y * Z + z for r in range(reps) for y in range(Y)] for z in range(Z)]
-    done = lax.all_to_all(pieces, ("rep", "row"), 0, 0, axis_index_groups=back, tiled=True)
+    calls = 2
+    step = part // calls
+    done = []
+    for c in range(calls):
+        at = slice(c * step, (c + 1) * step)
+        sigma = sigma_block(table, idx[at], weights[at], alpha_term[:, at])
+        if c + 1 < calls:
+            sigma, idx = lax.optimization_barrier((sigma, idx))
+        pieces = sigma.reshape(Y, own_rows, step)
+        pieces = jnp.concatenate([pieces] * reps, axis=0)
+        done.append(
+            lax.all_to_all(pieces, ("rep", "row"), 0, 0, axis_index_groups=back, tiled=True)
+        )
+    done = jnp.concatenate(done, axis=2)
     return done.reshape(parts, own_rows, part).transpose(1, 0, 2).reshape(own_rows, betas)
 
 

time: 221 us -> 212 us (0.959); the launches traced: 220 us -> 209 us
  blocking collectives: 73 us -> 18.9 us
  starting transfers between devices: 25.5 us -> 45.2 us
  waiting for transfers between devices: 52.5 us -> 64.2 us
  Pallas kernels: 44.9 us -> 53.1 us
    all_to_all x0 -> x2, waiting for transfers between devices: none -> 44.3 us  [the longest x1 22.5 us: per_device(): lax.all_to_all(alpha_term, 'row', 0, 0, axis_index_groups=along_z)]
    all_to_all x1 -> x0, blocking collectives: 37.8 us -> none  [per_device(): lax.all_to_all(alpha_term, 'row', 0, 0, axis_index_groups=along_z)]
    all_gather x1, waiting for transfers between devices: 34.2 us -> 0.01 us  [per_device(): lax.all_gather(pack_rows(coeffs, row // Z), ('row', 'col'), axis=0, axis_...]
    all_to_all x0 -> x2, starting transfers between devices: none -> 21.5 us  [the longest x1 13.4 us: per_device(): lax.all_to_all(pieces, ('rep', 'row'), 0, 0, axis_index_groups=back, tile...]
    all_to_all x1, blocking collectives: 35.2 us -> 18.9 us  [per_device(): lax.all_to_all(pieces, ('rep', 'row'), 0, 0, axis_index_groups=back, tile...]
    pallas_call x1 -> x3, Pallas kernels: 42.9 us -> 51.1 us  [the longest x2 43.4 us: sigma_block(): pl.pallas_call(pick_kernel, in_specs=[pl.BlockSpec(memory_space=pltpu.VME...]
    slice x0 -> x4, local copies, waits for them, and re-layouts: none -> 3.28 us  [per_device(): sigma = sigma_block(table, idx[at], weights[at], alpha_term[:, at])]
    unnamed x4, local copies, waits for them, and re-layouts: 2.78 us -> 0.01 us
  transfers between devices with their start and end apart: 4 -> 5, of which waited for: 3 -> 4; matrix products, arithmetic and copies ran while one was open for 3% -> 5% of each run, Pallas kernels for 0% -> 0%
where the time goes in v5:
time: 212 us; the launch traced here: 209 us
  waiting for transfers between devices  64.2 us (30%)
  Pallas kernels  53.1 us (25%)
  starting transfers between devices  45.2 us (21%)
  blocking collectives  18.9 us (9%)
  between operations  13.6 us (6%)
  local copies, waits for them, and re-layouts  9.23 us (4%)
  other arithmetic  4.23 us (2%)
    pallas_call x2, Pallas kernels, sigma_block(): pl.pallas_call(pick_kernel, in_specs=[pl.BlockSpec(memory_space=pltpu.VME...  43.4 us
    all_to_all x1, waiting for transfers between devices, per_device(): lax.all_to_all(alpha_term, 'row', 0, 0, axis_index_groups=along_z)  22.5 us
    all_to_all x1, waiting for transfers between devices, per_device(): lax.all_to_all(pieces, ('rep', 'row'), 0, 0, axis_index_groups=back, tile...  21.7 us
    all_to_all x1, blocking collectives, per_device(): lax.all_to_all(pieces, ('rep', 'row'), 0, 0, axis_index_groups=back, tile...  18.9 us
    ppermute x1, starting transfers between devices, per_device(): got = lax.ppermute(sent, 'rep', [(0, 1), (1, 0)])  14.8 us
    all_to_all x1, waiting for transfers between devices, per_device(): columns = lax.all_to_all(pieces, 'row', 0, 0).reshape(strings, small)  13.5 us
    all_to_all x1, starting transfers between devices, per_device(): lax.all_to_all(pieces, ('rep', 'row'), 0, 0, axis_index_groups=back, tile...  13.4 us
    all_to_all x1, starting transfers between devices, per_device(): columns = lax.all_to_all(pieces, 'row', 0, 0).reshape(strings, small)  8.81 us
  transfers between devices with their start and end apart: 5, of which 4 were waited for; matrix products, arithmetic and copies ran while one was open for 5% of the time, Pallas kernels for 0%

profile of v5, /device:TPU:32, one launch (start us, length us, event | category | flops | bytes accessed | tf_op | source)
XLA Modules:
  0.0 208.7 jit_solution(11586025974775050063)
XLA Ops:
  6.5 0.0 copy-start
  6.5 0.0 all-gather.3.cloned.1.call-start
  6.5 2.0 pack_rows.1
  8.5 0.0 all-gather.3.cloned.1.call-update
  8.6 1.0 constant_dynamic-slice_fusion.1
  9.5 1.0 constant_dynamic-slice_fusion.3
  10.5 14.8 %collective-permute-start = (f32[32,1536]{1,0:T(8,128)S(1)}, f32[32,1536]{1,0:T(8,128)S(1)}, u32[]{:S(2)}, u32[]{:S(2)}) collective-permute-start(f32[32,1536]{1,0:T(8,128)S(1)} %pad_maximum_fusion), channel_id=1, source_target_pairs={{0,1},{1,0},{2,3},{3,2},{4,5},{5,4},{6,7},{7,6},{8,9},{9,8},{10,11... | collective-permute-start | bytes 589832 | tf_op jit(solution)/shard_map/ppermute | solution.py:232
  25.4 0.9 constant_dynamic-slice_fusion
  26.3 0.3 reshape.29
  26.6 0.9 copy.43
  27.5 8.8 %all-to-all-start = ((bf16[32,16,192]{2,1,0:T(8,128)(2,1)}), bf16[32,16,192]{2,1,0:T(8,128)(2,1)S(1)}, u32[]{:S(2)}, u32[]{:S(2)}) async-start(bf16[32,16,192]{2,1,0:T(8,128)(2,1)} %copy.43), calls=%async_computation | async-start | bytes 524288 | tf_op jit(solution)/shard_map/all_to_all | solution.py:219
  36.3 6.4 %collective-permute-done = f32[32,1536]{1,0:T(8,128)S(1)} collective-permute-done((f32[32,1536]{1,0:T(8,128)S(1)}, f32[32,1536]{1,0:T(8,128)S(1)}, u32[]{:S(2)}, u32[]{:S(2)}) %collective-permute-start) | collective-permute-done | bytes 196640 | tf_op jit(solution)/shard_map/ppermute | solution.py:232
  42.8 0.3 copy.40
  43.1 0.3 copy.41
  43.4 13.5 %all-to-all-done = bf16[32,16,192]{2,1,0:T(8,128)(2,1)S(1)} async-done(((bf16[32,16,192]{2,1,0:T(8,128)(2,1)}), bf16[32,16,192]{2,1,0:T(8,128)(2,1)S(1)}, u32[]{:S(2)}, u32[]{:S(2)}) %all-to-all-start) | async-done | bytes 196640 | tf_op jit(solution)/shard_map/all_to_all | solution.py:219
  56.8 0.0 copy-done
  56.8 0.3 convolution_bitcast_fusion
  57.2 0.2 copy.44
  57.4 0.9 copy.45
  58.3 8.1 %all-to-all-start.1 = ((f32[8,4,16,192]{3,2,1,0:T(8,128)}), f32[8,4,16,192]{3,2,1,0:T(8,128)S(1)}, u32[]{:S(2)}, u32[]{:S(2)}) async-start(f32[8,4,16,192]{3,2,1,0:T(8,128)} %copy.45), calls=%async_computation.1 | async-start | bytes 1048576 | tf_op jit(solution)/shard_map/all_to_all | solution.py:222
  66.4 0.6 subtract_bitcast_fusion
  67.0 0.8 slice.33.idx_ref
  67.7 0.6 broadcast_select_fusion.1
  68.4 0.3 maximum_bitcast_fusion
  68.6 0.9 fusion.1
  69.6 22.5 %all-to-all-done.1 = f32[8,4,16,192]{3,2,1,0:T(8,128)S(1)} async-done(((f32[8,4,16,192]{3,2,1,0:T(8,128)}), f32[8,4,16,192]{3,2,1,0:T(8,128)S(1)}, u32[]{:S(2)}, u32[]{:S(2)}) %all-to-all-start.1) | async-done | bytes 393248 | tf_op jit(solution)/shard_map/all_to_all | solution.py:222
  92.1 0.3 copy.46
  92.4 0.2 reshape.32
  92.6 0.8 fusion.2
  93.4 0.0 all-gather.3.cloned.1.call-done
  93.4 7.6 %build_table.1.table = f32[49152,128]{1,0:T(8,128)S(1)} custom-call(bf16[4,8,1536,128]{3,2,1,0:T(8,128)(2,1)} %bitcast.24), custom_call_target="tpu_custom_call" | custom-call | flops 6442450944 | bytes 12582912 | tf_op jit(solution)/shard_map/build_table/pallas_call | solution.py:103
  101.0 21.7 %sigma_block.2 = bf16[64,768]{1,0:T(8,128)(2,1)} custom-call(f32[49152,128]{1,0:T(8,128)S(1)} %build_table.1.table, s32[768,32]{1,0:T(8,128)} %slice.33.idx_ref, f32[768,64]{1,0:T(8,128)} %get-tuple-element.12.w_ref, f32[64,768]{1,0:T(8,128)} %get-tuple-element.18.alpha_ref), custom_call_target="tpu_custom_call" | custom-call | flops 125829120 | bytes 125829120 | tf_op jit(solution)/shard_map/sigma_block/pallas_call | solution.py:173
  122.8 0.0 copy-start.1
  122.8 0.8 slice.29.idx_ref
  123.6 21.7 %sigma_block.3 = bf16[64,768]{1,0:T(8,128)(2,1)} custom-call(f32[49152,128]{1,0:T(8,128)S(1)} %build_table.1.table, s32[768,32]{1,0:T(8,128)} %slice.29.idx_ref, f32[768,64]{1,0:T(8,128)} %get-tuple-element.11.w_ref, f32[64,768]{1,0:T(8,128)} %get-tuple-element.17.alpha_ref), custom_call_target="tpu_custom_call" | custom-call | flops 125829120 | bytes 125829120 | tf_op jit(solution)/shard_map/sigma_block/pallas_call | solution.py:173
  145.3 1.7 pad_maximum_fusion.3
  147.0 13.4 %all-to-all-start.3 = ((bf16[8,16,768]{2,1,0:T(8,128)(2,1)}), bf16[8,16,768]{2,1,0:T(8,128)(2,1)S(1)}, u32[]{:S(2)}, u32[]{:S(2)}) async-start(bf16[8,16,768]{2,1,0:T(8,128)(2,1)} %pad_maximum_fusion.3), calls=%async_computation.3 | async-start | bytes 393216 | tf_op jit(solution)/shard_map/all_to_all | solution.py:264
  160.4 0.0 copy-done.1
  160.4 21.7 %all-to-all-done.3 = bf16[8,16,768]{2,1,0:T(8,128)(2,1)S(1)} async-done(((bf16[8,16,768]{2,1,0:T(8,128)(2,1)}), bf16[8,16,768]{2,1,0:T(8,128)(2,1)S(1)}, u32[]{:S(2)}, u32[]{:S(2)}) %all-to-all-start.3) | async-done | bytes 196640 | tf_op jit(solution)/shard_map/all_to_all | solution.py:264
  182.1 18.9 %all_to_all.20 = bf16[8,16,768]{2,1,0:T(8,128)(2,1)S(1)} all-to-all(bf16[8,16,768]{2,1,0:T(8,128)(2,1)S(1)} %pad_maximum_fusion.2), channel_id=1, replica_groups={{0,128,256,384,1,129,257,385},{16,144,272,400,17,145,273,401},{32,160,2..., dimensions={0} | all-to-all | bytes 393216 | tf_op jit(solution)/shard_map/all_to_all | solution.py:264
  201.0 0.8 copy.48
  (6 shorter events, 0.1 us)
Async XLA Ops:
  6.5 50.3 %copy-start = (bf16[512,512]{1,0:T(8,128)(2,1)S(1)}, bf16[512,512]{1,0:T(8,128)(2,1)}, u32[]{:S(2)}) copy-start(bf16[512,512]{1,0:T(8,128)(2,1)} %param.5) | copy-start | bytes 1572868
  6.5 86.9 %all-gather.3.cloned.1.call-start = ((), (), s32[]{:S(2)}) async-start(), calls=%async_computation.4 | async-start | bytes 12976128 | tf_op jit(solution)/shard_map/all_gather | solution.py:213
  10.5 32.2 %collective-permute-start = (f32[32,1536]{1,0:T(8,128)S(1)}, f32[32,1536]{1,0:T(8,128)S(1)}, u32[]{:S(2)}, u32[]{:S(2)}) collective-permute-start(f32[32,1536]{1,0:T(8,128)S(1)} %pad_maximum_fusion), channel_id=1, source_target_pairs={{0,1},{1,0},{2,3},{3,2},{4,5},{5,4},{6,7},{7,6},{8,9},{9,8},{10,11... | collective-permute-start | bytes 589832 | tf_op jit(solution)/shard_map/ppermute | solution.py:232
  27.5 29.3 %all-to-all-start = ((bf16[32,16,192]{2,1,0:T(8,128)(2,1)}), bf16[32,16,192]{2,1,0:T(8,128)(2,1)S(1)}, u32[]{:S(2)}, u32[]{:S(2)}) async-start(bf16[32,16,192]{2,1,0:T(8,128)(2,1)} %copy.43), calls=%async_computation | async-start | bytes 524288 | tf_op jit(solution)/shard_map/all_to_all | solution.py:219
  58.3 33.9 %all-to-all-start.1 = ((f32[8,4,16,192]{3,2,1,0:T(8,128)}), f32[8,4,16,192]{3,2,1,0:T(8,128)S(1)}, u32[]{:S(2)}, u32[]{:S(2)}) async-start(f32[8,4,16,192]{3,2,1,0:T(8,128)} %copy.45), calls=%async_computation.1 | async-start | bytes 1048576 | tf_op jit(solution)/shard_map/all_to_all | solution.py:222
  122.8 37.6 %copy-start.1 = (bf16[64,768]{1,0:T(8,128)(2,1)S(1)}, bf16[64,768]{1,0:T(8,128)(2,1)}, u32[]{:S(2)}) copy-start(bf16[64,768]{1,0:T(8,128)(2,1)} %sigma_block.2) | copy-start | bytes 294916
  147.0 35.2 %all-to-all-start.3 = ((bf16[8,16,768]{2,1,0:T(8,128)(2,1)}), bf16[8,16,768]{2,1,0:T(8,128)(2,1)S(1)}, u32[]{:S(2)}, u32[]{:S(2)}) async-start(bf16[8,16,768]{2,1,0:T(8,128)(2,1)} %pad_maximum_fusion.3), calls=%async_computation.3 | async-start | bytes 393216 | tf_op jit(solution)/shard_map/all_to_all | solution.py:264
Sparse Core Ops, SparseCore 0:
  10.5 82.8 all-gather.2

commit v6 on v5

--- a/solution.py
+++ b/solution.py
@@ -40,7 +40,7 @@
     )(turn.reshape(1), coeffs)
 
 
-def table_kernel(chunk, packed_ref, table, stage, spread, sems):
+def fill_table(chunk, packed_ref, table, stage, spread, sems):
     _, classes, rows, _ = packed_ref.shape
     per_class = rows // chunk
     chunks = classes * per_class
@@ -97,28 +97,11 @@
                     table[pl.ds(to, piece), :] = turned[:, lanes : lanes + LANES]
 
 
-def build_table(packed, chunk=768, depth=4):
-    _, classes, rows, _ = packed.shape
-    pairs = classes * rows * Y
-    return pl.pallas_call(
-        functools.partial(table_kernel, chunk),
-        in_specs=[pl.BlockSpec(memory_space=pl.ANY)],
-        out_specs=pl.BlockSpec(memory_space=pltpu.VMEM),
-        out_shape=pltpu.VMEM((pairs, LANES), jnp.float32),
-        scratch_shapes=[
-            pltpu.VMEM((depth, Y, chunk, LANES), jnp.bfloat16),
-            pltpu.VMEM((Y // 2, 2 * LANES, 2 * LANES), jnp.bfloat16),
-            pltpu.SemaphoreType.DMA((depth,)),
-        ],
-        compiler_params=pltpu.CompilerParams(vmem_limit_bytes=30 * 2**20),
-        cost_estimate=pl.CostEstimate(
-            flops=2 * pairs * LANES * Y * LANES, bytes_accessed=packed.size * 2, transcendentals=0
-        ),
-        name="build_table",
-    )(packed)
-
-
-def pick_kernel(table, idx_ref, w_ref, alpha_ref, out_ref, acc_ref, near, near_sems):
+def sigma_kernel(
+    chunk,
+    idx_ref, w_ref, alpha_ref, packed_ref, out_ref,
+    table, stage, spread, acc_ref, near, sems, near_sems,
+):
     buffers, batch, slots = near.shape
     targets = w_ref.shape[0]
     rounds = targets // (buffers * batch)
@@ -132,8 +115,10 @@
     for b in range(buffers):
         bring(0, b).start()
 
+    fill_table(chunk, packed_ref, table, stage, spread, sems)
+
     lane_row = lax.broadcasted_iota(jnp.int32, (8, LANES), 0)
-    low_lane = lax.broadcasted_iota(jnp.int32, (8, LANES), 1) < LANES // 2
+    lane_slot = lax.shift_right_logical(lax.broadcasted_iota(jnp.int32, (8, LANES), 1), 6) * slots
 
     @pl.loop(0, rounds)
     def _(r):
@@ -149,9 +134,10 @@
                         row = table[pl.ds(near[b, g + k, q], 1), :]
                         row = jnp.broadcast_to(row, (8, LANES))
                         picked = row if k == 0 else jnp.where(lane_row == k, row, picked)
-                    low = jnp.broadcast_to(weights[:, q : q + 1], (8, LANES))
-                    high = jnp.broadcast_to(weights[:, slots + q : slots + q + 1], (8, LANES))
-                    total = total + picked * jnp.where(low_lane, low, high)
+                    weight = jnp.take_along_axis(
+                        weights, lane_slot + q, axis=1, mode="promise_in_bounds"
+                    )
+                    total = total + picked * weight
                 acc_ref[pl.ds(base, 8), :] = total
 
             @pl.when(r + 1 < rounds)
@@ -166,33 +152,38 @@
         out_ref[:, pl.ds(at, LANES)] = total.astype(out_ref.dtype)
 
 
-def sigma_block(table, idx, weights, alpha_term, buffers=2, batch=32):
+def sigma_block(idx, weights, alpha_term, packed, chunk=768, depth=4, buffers=2, batch=32):
     targets, slots = idx.shape
     alphas = alpha_term.shape[0]
-    table = pltpu.with_memory_space_constraint(table, pltpu.VMEM)
+    _, classes, rows, _ = packed.shape
+    pairs = classes * rows * Y
     return pl.pallas_call(
-        pick_kernel,
+        functools.partial(sigma_kernel, chunk),
         in_specs=[
-            pl.BlockSpec(memory_space=pltpu.VMEM),
             pl.BlockSpec(memory_space=pl.ANY),
             pl.BlockSpec(memory_space=pltpu.VMEM),
             pl.BlockSpec(memory_space=pltpu.VMEM),
+            pl.BlockSpec(memory_space=pl.ANY),
         ],
         out_specs=pl.BlockSpec(memory_space=pltpu.VMEM),
         out_shape=jax.ShapeDtypeStruct((alphas, targets), jnp.bfloat16),
         scratch_shapes=[
+            pltpu.VMEM((pairs, LANES), jnp.float32),
+            pltpu.VMEM((depth, Y, chunk, LANES), jnp.bfloat16),
+            pltpu.VMEM((Y // 2, 2 * LANES, 2 * LANES), jnp.bfloat16),
             pltpu.VMEM((targets, LANES), jnp.float32),
             pltpu.SMEM((buffers, batch, slots), jnp.int32),
+            pltpu.SemaphoreType.DMA((depth,)),
             pltpu.SemaphoreType.DMA((buffers,)),
         ],
-        compiler_params=pltpu.CompilerParams(vmem_limit_bytes=30 * 2**20),
+        compiler_params=pltpu.CompilerParams(vmem_limit_bytes=56 * 2**20),
         cost_estimate=pl.CostEstimate(
-            flops=40 * targets * slots * LANES,
-            bytes_accessed=40 * targets * slots * LANES,
+            flops=2 * alphas * targets * slots + 2 * pairs * LANES * Y * LANES,
+            bytes_accessed=packed.size * 2 + targets * slots * 8 + alphas * targets * 6,
             transcendentals=0,
         ),
         name="sigma_block",
-    )(table, idx, weights, alpha_term)
+    )(idx, weights, alpha_term, packed)
 
 
 def per_device(coeffs, alpha_coupling, parent_string_index, excitation_weight):
@@ -244,26 +235,14 @@
     halves = idx // (betas // 2)
     upper = (halves & 1) == 1
     idx = (idx - ((halves + 1) >> 1) * (betas // 2)).T
-    weights = jnp.concatenate(
-        [jnp.where(upper, 0.0, weights), jnp.where(upper, weights, 0.0)], axis=0
-    ).T
-
-    table = build_table(packed)
+    low, high = jnp.where(upper, 0.0, weights), jnp.where(upper, weights, 0.0)
+    weights = jnp.concatenate([low, high] * (LANES // (2 * low.shape[0])), axis=0).T
+
+    sigma = sigma_block(idx, weights, alpha_term, packed)
+    pieces = sigma.reshape(Y, own_rows, part)
+    pieces = jnp.concatenate([pieces] * reps, axis=0)
     back = [[r * Y * Z + y * Z + z for r in range(reps) for y in range(Y)] for z in range(Z)]
-    calls = 2
-    step = part // calls
-    done = []
-    for c in range(calls):
-        at = slice(c * step, (c + 1) * step)
-        sigma = sigma_block(table, idx[at], weights[at], alpha_term[:, at])
-        if c + 1 < calls:
-            sigma, idx = lax.optimization_barrier((sigma, idx))
-        pieces = sigma.reshape(Y, own_rows, step)
-        pieces = jnp.concatenate([pieces] * reps, axis=0)
-        done.append(
-            lax.all_to_all(pieces, ("rep", "row"), 0, 0, axis_index_groups=back, tiled=True)
-        )
-    done = jnp.concatenate(done, axis=2)
+    done = lax.all_to_all(pieces, ("rep", "row"), 0, 0, axis_index_groups=back, tiled=True)
     return done.reshape(parts, own_rows, part).transpose(1, 0, 2).reshape(own_rows, betas)
 
 

time: 212 us -> 196 us (0.925)
  blocking collectives: 18.9 us -> 43.6 us
  waiting for transfers between devices: 64.2 us -> 42.1 us
  starting transfers between devices: 45.2 us -> 31.7 us
  Pallas kernels: 53.1 us -> 49.3 us
  local copies, waits for them, and re-layouts: 9.23 us -> 6.64 us
    all_to_all x1, blocking collectives: 18.9 us -> 43.6 us  [per_device(): lax.all_to_all(pieces, ('rep', 'row'), 0, 0, axis_index_groups=back, tile...]
    all_to_all x1 -> x0, waiting for transfers between devices: 21.7 us -> none  [per_device(): lax.all_to_all(pieces, ('rep', 'row'), 0, 0, axis_index_groups=back, tile...]
    all_to_all x1 -> x0, starting transfers between devices: 13.4 us -> none  [per_device(): lax.all_to_all(pieces, ('rep', 'row'), 0, 0, axis_index_groups=back, tile...]
    pallas_call x3 -> x1, Pallas kernels: 51.1 us -> 47.3 us  [sigma_block(): pl.pallas_call(functools.partial(sigma_kernel, chunk), in_specs=[pl.Block...]
    slice x4 -> x0, local copies, waits for them, and re-layouts: 3.28 us -> none  [per_device(): sigma = sigma_block(table, idx[at], weights[at], alpha_term[:, at])]
  transfers between devices with their start and end apart: 5 -> 4, of which waited for: 4 -> 4; matrix products, arithmetic and copies ran while one was open for 5% -> 6% of each run, Pallas kernels for 0% -> 0%
where the time goes in v6:
time: 196 us; the launch traced here: 193 us
  Pallas kernels  49.3 us (25%)
  blocking collectives  43.6 us (22%)
  waiting for transfers between devices  42.1 us (21%)
  starting transfers between devices  31.7 us (16%)
  between operations  13.5 us (7%)
  local copies, waits for them, and re-layouts  6.64 us (3%)
  other arithmetic  5.82 us (3%)
    pallas_call x1, Pallas kernels, sigma_block(): pl.pallas_call(functools.partial(sigma_kernel, chunk), in_specs=[pl.Block...  47.3 us
    all_to_all x1, blocking collectives, per_device(): lax.all_to_all(pieces, ('rep', 'row'), 0, 0, axis_index_groups=back, tile...  43.6 us
    all_to_all x1, waiting for transfers between devices, per_device(): lax.all_to_all(alpha_term, 'row', 0, 0, axis_index_groups=along_z)  21.5 us
    ppermute x1, starting transfers between devices, per_device(): got = lax.ppermute(sent, 'rep', [(0, 1), (1, 0)])  14.8 us
    all_to_all x1, waiting for transfers between devices, per_device(): columns = lax.all_to_all(pieces, 'row', 0, 0).reshape(strings, small)  14 us
    all_to_all x1, starting transfers between devices, per_device(): columns = lax.all_to_all(pieces, 'row', 0, 0).reshape(strings, small)  8.81 us
    all_to_all x1, starting transfers between devices, per_device(): lax.all_to_all(alpha_term, 'row', 0, 0, axis_index_groups=along_z)  8.1 us
    ppermute x1, waiting for transfers between devices, per_device(): got = lax.ppermute(sent, 'rep', [(0, 1), (1, 0)])  6.46 us
  transfers between devices with their start and end apart: 4, of which 4 were waited for; matrix products, arithmetic and copies ran while one was open for 6% of the time, Pallas kernels for 0%

profile of v6, /device:TPU:32, one launch (start us, length us, event | category | flops | bytes accessed | tf_op | source)
XLA Modules:
  0.0 193.0 jit_solution(9269163243185168281)
XLA Ops:
  6.5 0.0 copy-start
  6.5 0.0 all-gather.3.cloned.1.call-start
  6.5 2.0 %pack_rows.1 = bf16[1536,128]{1,0:T(8,128)(2,1)} custom-call(s32[1]{0:T(128)} %bitcast.8.turn_ref, bf16[16,12288]{1,0:T(8,128)(2,1)} %in_ref.1), custom_call_target="tpu_custom_call" | custom-call | tf_op jit(solution)/shard_map/pack_rows/pallas_call | solution.py:31
  8.5 0.0 all-gather.3.cloned.1.call-update
  8.6 1.0 constant_dynamic-slice_fusion.1
  9.6 1.0 constant_dynamic-slice_fusion.3
  10.5 14.8 %collective-permute-start = (f32[32,1536]{1,0:T(8,128)S(1)}, f32[32,1536]{1,0:T(8,128)S(1)}, u32[]{:S(2)}, u32[]{:S(2)}) collective-permute-start(f32[32,1536]{1,0:T(8,128)S(1)} %pad_maximum_fusion.1), channel_id=1, source_target_pairs={{0,1},{1,0},{2,3},{3,2},{4,5},{5,4},{6,7},{7,6},{8,9},{9,8},{10,11... | collective-permute-start | bytes 589832 | tf_op jit(solution)/shard_map/ppermute | solution.py:223
  25.4 0.9 constant_dynamic-slice_fusion
  26.3 0.3 reshape.24
  26.6 0.9 copy.43
  27.5 8.8 %all-to-all-start = ((bf16[32,16,192]{2,1,0:T(8,128)(2,1)}), bf16[32,16,192]{2,1,0:T(8,128)(2,1)S(1)}, u32[]{:S(2)}, u32[]{:S(2)}) async-start(bf16[32,16,192]{2,1,0:T(8,128)(2,1)} %copy.43), calls=%async_computation | async-start | bytes 524288 | tf_op jit(solution)/shard_map/all_to_all | solution.py:210
  36.3 6.5 %collective-permute-done = f32[32,1536]{1,0:T(8,128)S(1)} collective-permute-done((f32[32,1536]{1,0:T(8,128)S(1)}, f32[32,1536]{1,0:T(8,128)S(1)}, u32[]{:S(2)}, u32[]{:S(2)}) %collective-permute-start) | collective-permute-done | bytes 196640 | tf_op jit(solution)/shard_map/ppermute | solution.py:223
  42.8 14.0 %all-to-all-done = bf16[32,16,192]{2,1,0:T(8,128)(2,1)S(1)} async-done(((bf16[32,16,192]{2,1,0:T(8,128)(2,1)}), bf16[32,16,192]{2,1,0:T(8,128)(2,1)S(1)}, u32[]{:S(2)}, u32[]{:S(2)}) %all-to-all-start) | async-done | bytes 196640 | tf_op jit(solution)/shard_map/all_to_all | solution.py:210
  56.8 0.0 copy-done
  56.8 0.3 convolution_bitcast_fusion
  57.2 0.2 copy.44
  57.4 0.8 copy.45
  58.2 8.1 %all-to-all-start.1 = ((f32[8,4,16,192]{3,2,1,0:T(8,128)}), f32[8,4,16,192]{3,2,1,0:T(8,128)S(1)}, u32[]{:S(2)}, u32[]{:S(2)}) async-start(f32[8,4,16,192]{3,2,1,0:T(8,128)} %copy.45), calls=%async_computation.1 | async-start | bytes 1048576 | tf_op jit(solution)/shard_map/all_to_all | solution.py:213
  66.4 0.3 copy.40
  66.6 0.3 copy.41
  66.9 0.6 broadcast_select_fusion.1
  67.5 1.6 maximum_bitcast_fusion.w_ref
  69.1 1.6 subtract_bitcast_fusion.idx_ref
  70.6 21.5 %all-to-all-done.1 = f32[8,4,16,192]{3,2,1,0:T(8,128)S(1)} async-done(((f32[8,4,16,192]{3,2,1,0:T(8,128)}), f32[8,4,16,192]{3,2,1,0:T(8,128)S(1)}, u32[]{:S(2)}, u32[]{:S(2)}) %all-to-all-start.1) | async-done | bytes 393248 | tf_op jit(solution)/shard_map/all_to_all | solution.py:213
  92.1 0.3 copy.46
  92.4 0.9 reshape.27.alpha_ref
  93.3 0.1 all-gather.3.cloned.1.call-done
  93.4 47.3 %sigma_block.1 = bf16[64,1536]{1,0:T(8,128)(2,1)} custom-call(s32[1536,32]{1,0:T(8,128)} %subtract_bitcast_fusion.idx_ref, f32[1536,128]{1,0:T(8,128)} %maximum_bitcast_fusion.w_ref, f32[64,1536]{1,0:T(8,128)} %reshape.27.alpha_ref, bf16[4,8,1536,128]{3,2,1,0:T(8,128)(2,1)} %bitcast.28), custom_call_target="tpu_custom_call" | custom-call | flops 6448742400 | bytes 13565952 | tf_op jit(solution)/shard_map/sigma_block/pallas_call | solution.py:160
  140.8 1.1 pad_maximum_fusion
  141.8 43.6 %all_to_all.15 = bf16[8,16,1536]{2,1,0:T(8,128)(2,1)S(1)} all-to-all(bf16[8,16,1536]{2,1,0:T(8,128)(2,1)S(1)} %pad_maximum_fusion), channel_id=1, replica_groups={{0,128,256,384,1,129,257,385},{16,144,272,400,17,145,273,401},{32,160,2..., dimensions={0} | all-to-all | bytes 786432 | tf_op jit(solution)/shard_map/all_to_all | solution.py:245
  185.4 0.8 copy.48
  (4 shorter events, 0.1 us)
Async XLA Ops:
  6.5 50.3 %copy-start = (bf16[512,512]{1,0:T(8,128)(2,1)S(1)}, bf16[512,512]{1,0:T(8,128)(2,1)}, u32[]{:S(2)}) copy-start(bf16[512,512]{1,0:T(8,128)(2,1)} %param.5) | copy-start | bytes 1572868
  6.5 86.9 %all-gather.3.cloned.1.call-start = ((), (), s32[]{:S(2)}) async-start(), calls=%async_computation.3 | async-start | bytes 12976128 | tf_op jit(solution)/shard_map/all_gather | solution.py:204
  10.5 32.2 %collective-permute-start = (f32[32,1536]{1,0:T(8,128)S(1)}, f32[32,1536]{1,0:T(8,128)S(1)}, u32[]{:S(2)}, u32[]{:S(2)}) collective-permute-start(f32[32,1536]{1,0:T(8,128)S(1)} %pad_maximum_fusion.1), channel_id=1, source_target_pairs={{0,1},{1,0},{2,3},{3,2},{4,5},{5,4},{6,7},{7,6},{8,9},{9,8},{10,11... | collective-permute-start | bytes 589832 | tf_op jit(solution)/shard_map/ppermute | solution.py:223
  27.5 29.3 %all-to-all-start = ((bf16[32,16,192]{2,1,0:T(8,128)(2,1)}), bf16[32,16,192]{2,1,0:T(8,128)(2,1)S(1)}, u32[]{:S(2)}, u32[]{:S(2)}) async-start(bf16[32,16,192]{2,1,0:T(8,128)(2,1)} %copy.43), calls=%async_computation | async-start | bytes 524288 | tf_op jit(solution)/shard_map/all_to_all | solution.py:210
  58.2 33.9 %all-to-all-start.1 = ((f32[8,4,16,192]{3,2,1,0:T(8,128)}), f32[8,4,16,192]{3,2,1,0:T(8,128)S(1)}, u32[]{:S(2)}, u32[]{:S(2)}) async-start(f32[8,4,16,192]{3,2,1,0:T(8,128)} %copy.45), calls=%async_computation.1 | async-start | bytes 1048576 | tf_op jit(solution)/shard_map/all_to_all | solution.py:213
Sparse Core Ops, SparseCore 0:
  10.5 82.9 all-gather.2

commit v7 on v6

--- a/solution.py
+++ b/solution.py
@@ -144,15 +144,18 @@
             def _():
                 bring(r + 1, b).start()
 
-    alphas = out_ref.shape[0]
+    alphas = alpha_ref.shape[0]
+    pieces, piece_rows, _ = out_ref.shape
     for at in range(0, targets, LANES):
         turned = acc_ref[pl.ds(at, LANES), :].T
         beta_term = turned[:alphas, :] + turned[alphas:, :]
-        total = alpha_ref[:, pl.ds(at, LANES)] + beta_term
-        out_ref[:, pl.ds(at, LANES)] = total.astype(out_ref.dtype)
-
-
-def sigma_block(idx, weights, alpha_term, packed, chunk=768, depth=4, buffers=2, batch=32):
+        total = (alpha_ref[:, pl.ds(at, LANES)] + beta_term).astype(out_ref.dtype)
+        for p in range(pieces):
+            first = p * piece_rows % alphas
+            out_ref[p, :, pl.ds(at, LANES)] = total[first : first + piece_rows, :]
+
+
+def sigma_block(pieces, idx, weights, alpha_term, packed, chunk=768, depth=4, buffers=4, batch=16):
     targets, slots = idx.shape
     alphas = alpha_term.shape[0]
     _, classes, rows, _ = packed.shape
@@ -160,13 +163,13 @@
     return pl.pallas_call(
         functools.partial(sigma_kernel, chunk),
         in_specs=[
+            pl.BlockSpec(memory_space=pltpu.VMEM),
+            pl.BlockSpec(memory_space=pltpu.VMEM),
+            pl.BlockSpec(memory_space=pltpu.VMEM),
             pl.BlockSpec(memory_space=pl.ANY),
-            pl.BlockSpec(memory_space=pltpu.VMEM),
-            pl.BlockSpec(memory_space=pltpu.VMEM),
-            pl.BlockSpec(memory_space=pl.ANY),
         ],
         out_specs=pl.BlockSpec(memory_space=pltpu.VMEM),
-        out_shape=jax.ShapeDtypeStruct((alphas, targets), jnp.bfloat16),
+        out_shape=jax.ShapeDtypeStruct((pieces, alphas // Y, targets), jnp.bfloat16),
         scratch_shapes=[
             pltpu.VMEM((pairs, LANES), jnp.float32),
             pltpu.VMEM((depth, Y, chunk, LANES), jnp.bfloat16),
@@ -176,7 +179,7 @@
             pltpu.SemaphoreType.DMA((depth,)),
             pltpu.SemaphoreType.DMA((buffers,)),
         ],
-        compiler_params=pltpu.CompilerParams(vmem_limit_bytes=56 * 2**20),
+        compiler_params=pltpu.CompilerParams(vmem_limit_bytes=52 * 2**20),
         cost_estimate=pl.CostEstimate(
             flops=2 * alphas * targets * slots + 2 * pairs * LANES * Y * LANES,
             bytes_accessed=packed.size * 2 + targets * slots * 8 + alphas * targets * 6,
@@ -238,9 +241,7 @@
     low, high = jnp.where(upper, 0.0, weights), jnp.where(upper, weights, 0.0)
     weights = jnp.concatenate([low, high] * (LANES // (2 * low.shape[0])), axis=0).T
 
-    sigma = sigma_block(idx, weights, alpha_term, packed)
-    pieces = sigma.reshape(Y, own_rows, part)
-    pieces = jnp.concatenate([pieces] * reps, axis=0)
+    pieces = sigma_block(reps * Y, idx, weights, alpha_term, packed)
     back = [[r * Y * Z + y * Z + z for r in range(reps) for y in range(Y)] for z in range(Z)]
     done = lax.all_to_all(pieces, ("rep", "row"), 0, 0, axis_index_groups=back, tiled=True)
     return done.reshape(parts, own_rows, part).transpose(1, 0, 2).reshape(own_rows, betas)

time: 196 us -> 186 us (0.949); the launches traced: 193 us -> 185 us
  Pallas kernels: 49.3 us -> 42.8 us
    pallas_call x1, Pallas kernels: 47.3 us -> 40.8 us  [sigma_block(): pl.pallas_call(functools.partial(sigma_kernel, chunk), in_specs=[pl.Block...]
  transfers between devices with their start and end apart: 4 -> 4, of which waited for: 4 -> 4; matrix products, arithmetic and copies ran while one was open for 6% -> 5% of each run, Pallas kernels for 0% -> 0%
where the time goes in v7:
time: 186 us; the launch traced here: 185 us
  waiting for transfers between devices  43.7 us (23%)
  blocking collectives  43.6 us (23%)
  Pallas kernels  42.8 us (23%)
  starting transfers between devices  31.7 us (17%)
  between operations  13.5 us (7%)
  local copies, waits for them, and re-layouts  5.9 us (3%)
  other arithmetic  3.88 us (2%)
    all_to_all x1, blocking collectives, per_device(): lax.all_to_all(pieces, ('rep', 'row'), 0, 0, axis_index_groups=back, tile...  43.6 us
    pallas_call x1, Pallas kernels, sigma_block(): pl.pallas_call(functools.partial(sigma_kernel, chunk), in_specs=[pl.Block...  40.8 us
    all_to_all x1, waiting for transfers between devices, per_device(): lax.all_to_all(alpha_term, 'row', 0, 0, axis_index_groups=along_z)  22.3 us
    ppermute x1, starting transfers between devices, per_device(): got = lax.ppermute(sent, 'rep', [(0, 1), (1, 0)])  14.8 us
    all_to_all x1, waiting for transfers between devices, per_device(): columns = lax.all_to_all(pieces, 'row', 0, 0).reshape(strings, small)  14 us
    all_to_all x1, starting transfers between devices, per_device(): columns = lax.all_to_all(pieces, 'row', 0, 0).reshape(strings, small)  8.81 us
    all_to_all x1, starting transfers between devices, per_device(): lax.all_to_all(alpha_term, 'row', 0, 0, axis_index_groups=along_z)  8.1 us
    ppermute x1, waiting for transfers between devices, per_device(): got = lax.ppermute(sent, 'rep', [(0, 1), (1, 0)])  6.45 us
  transfers between devices with their start and end apart: 4, of which 4 were waited for; matrix products, arithmetic and copies ran while one was open for 5% of the time, Pallas kernels for 0%

profile of v7, /device:TPU:32, one launch (start us, length us, event | category | flops | bytes accessed | tf_op | source)
XLA Modules:
  0.0 185.4 jit_solution(9630482312361389417)
XLA Ops:
  6.5 0.0 copy-start
  6.5 0.0 all-gather.3.cloned.1.call-start
  6.5 2.0 %pack_rows.1 = bf16[1536,128]{1,0:T(8,128)(2,1)} custom-call(s32[1]{0:T(128)} %bitcast.8.turn_ref, bf16[16,12288]{1,0:T(8,128)(2,1)} %in_ref.1), custom_call_target="tpu_custom_call" | custom-call | tf_op jit(solution)/shard_map/pack_rows/pallas_call | solution.py:31
  8.5 0.0 all-gather.3.cloned.1.call-update
  8.6 1.0 constant_dynamic-slice_fusion.1
  9.5 1.0 constant_dynamic-slice_fusion.3
  10.5 14.8 %collective-permute-start = (f32[32,1536]{1,0:T(8,128)S(1)}, f32[32,1536]{1,0:T(8,128)S(1)}, u32[]{:S(2)}, u32[]{:S(2)}) collective-permute-start(f32[32,1536]{1,0:T(8,128)S(1)} %pad_maximum_fusion), channel_id=1, source_target_pairs={{0,1},{1,0},{2,3},{3,2},{4,5},{5,4},{6,7},{7,6},{8,9},{9,8},{10,11... | collective-permute-start | bytes 589832 | tf_op jit(solution)/shard_map/ppermute | solution.py:226
  25.4 0.9 constant_dynamic-slice_fusion
  26.3 0.3 reshape.21
  26.6 0.9 copy.42
  27.5 8.8 %all-to-all-start = ((bf16[32,16,192]{2,1,0:T(8,128)(2,1)}), bf16[32,16,192]{2,1,0:T(8,128)(2,1)S(1)}, u32[]{:S(2)}, u32[]{:S(2)}) async-start(bf16[32,16,192]{2,1,0:T(8,128)(2,1)} %copy.42), calls=%async_computation | async-start | bytes 524288 | tf_op jit(solution)/shard_map/all_to_all | solution.py:213
  36.3 6.5 %collective-permute-done = f32[32,1536]{1,0:T(8,128)S(1)} collective-permute-done((f32[32,1536]{1,0:T(8,128)S(1)}, f32[32,1536]{1,0:T(8,128)S(1)}, u32[]{:S(2)}, u32[]{:S(2)}) %collective-permute-start) | collective-permute-done | bytes 196640 | tf_op jit(solution)/shard_map/ppermute | solution.py:226
  42.8 14.0 %all-to-all-done = bf16[32,16,192]{2,1,0:T(8,128)(2,1)S(1)} async-done(((bf16[32,16,192]{2,1,0:T(8,128)(2,1)}), bf16[32,16,192]{2,1,0:T(8,128)(2,1)S(1)}, u32[]{:S(2)}, u32[]{:S(2)}) %all-to-all-start) | async-done | bytes 196640 | tf_op jit(solution)/shard_map/all_to_all | solution.py:213
  56.8 0.0 copy-done
  56.8 0.3 convolution_bitcast_fusion
  57.2 0.2 copy.43
  57.4 0.8 copy.44
  58.2 8.1 %all-to-all-start.1 = ((f32[8,4,16,192]{3,2,1,0:T(8,128)}), f32[8,4,16,192]{3,2,1,0:T(8,128)S(1)}, u32[]{:S(2)}, u32[]{:S(2)}) async-start(f32[8,4,16,192]{3,2,1,0:T(8,128)} %copy.44), calls=%async_computation.1 | async-start | bytes 1048576 | tf_op jit(solution)/shard_map/all_to_all | solution.py:216
  66.3 0.3 copy.39
  66.6 0.3 copy.40
  66.9 0.6 broadcast_select_fusion.1
  67.5 1.6 maximum_bitcast_fusion.w_ref
  69.1 0.6 subtract_bitcast_fusion.idx_ref
  69.8 22.3 %all-to-all-done.1 = f32[8,4,16,192]{3,2,1,0:T(8,128)S(1)} async-done(((f32[8,4,16,192]{3,2,1,0:T(8,128)}), f32[8,4,16,192]{3,2,1,0:T(8,128)S(1)}, u32[]{:S(2)}, u32[]{:S(2)}) %all-to-all-start.1) | async-done | bytes 393248 | tf_op jit(solution)/shard_map/all_to_all | solution.py:216
  92.1 0.3 copy.45
  92.4 0.2 reshape.24.alpha_ref
  92.6 0.8 all-gather.3.cloned.1.call-done
  93.4 40.8 %sigma_block.1 = bf16[8,16,1536]{2,1,0:T(8,128)(2,1)S(1)} custom-call(s32[1536,32]{1,0:T(8,128)S(1)} %subtract_bitcast_fusion.idx_ref, f32[1536,128]{1,0:T(8,128)} %maximum_bitcast_fusion.w_ref, f32[64,1536]{1,0:T(8,128)S(1)} %reshape.24.alpha_ref, bf16[4,8,1536,128]{3,2,1,0:T(8,128)(2,1)} %bitcast.26), custom_call_target="tpu_custom_call" | custom-call | flops 6448742400 | bytes 13565952 | tf_op jit(solution)/shard_map/sigma_block/pallas_call | solution.py:163
  134.2 43.6 %all_to_all.15 = bf16[8,16,1536]{2,1,0:T(8,128)(2,1)S(1)} all-to-all(bf16[8,16,1536]{2,1,0:T(8,128)(2,1)S(1)} %sigma_block.1), channel_id=1, replica_groups={{0,128,256,384,1,129,257,385},{16,144,272,400,17,145,273,401},{32,160,2..., dimensions={0} | all-to-all | bytes 786432 | tf_op jit(solution)/shard_map/all_to_all | solution.py:246
  177.8 0.8 copy.47
  (4 shorter events, 0.1 us)
Async XLA Ops:
  6.5 50.3 %copy-start = (bf16[512,512]{1,0:T(8,128)(2,1)S(1)}, bf16[512,512]{1,0:T(8,128)(2,1)}, u32[]{:S(2)}) copy-start(bf16[512,512]{1,0:T(8,128)(2,1)} %param.5) | copy-start | bytes 1572868
  6.5 86.9 %all-gather.3.cloned.1.call-start = ((), (), s32[]{:S(2)}) async-start(), calls=%async_computation.3 | async-start | bytes 12976128 | tf_op jit(solution)/shard_map/all_gather | solution.py:207
  10.5 32.2 %collective-permute-start = (f32[32,1536]{1,0:T(8,128)S(1)}, f32[32,1536]{1,0:T(8,128)S(1)}, u32[]{:S(2)}, u32[]{:S(2)}) collective-permute-start(f32[32,1536]{1,0:T(8,128)S(1)} %pad_maximum_fusion), channel_id=1, source_target_pairs={{0,1},{1,0},{2,3},{3,2},{4,5},{5,4},{6,7},{7,6},{8,9},{9,8},{10,11... | collective-permute-start | bytes 589832 | tf_op jit(solution)/shard_map/ppermute | solution.py:226
  27.5 29.3 %all-to-all-start = ((bf16[32,16,192]{2,1,0:T(8,128)(2,1)}), bf16[32,16,192]{2,1,0:T(8,128)(2,1)S(1)}, u32[]{:S(2)}, u32[]{:S(2)}) async-start(bf16[32,16,192]{2,1,0:T(8,128)(2,1)} %copy.42), calls=%async_computation | async-start | bytes 524288 | tf_op jit(solution)/shard_map/all_to_all | solution.py:213
  58.2 33.9 %all-to-all-start.1 = ((f32[8,4,16,192]{3,2,1,0:T(8,128)}), f32[8,4,16,192]{3,2,1,0:T(8,128)S(1)}, u32[]{:S(2)}, u32[]{:S(2)}) async-start(f32[8,4,16,192]{3,2,1,0:T(8,128)} %copy.44), calls=%async_computation.1 | async-start | bytes 1048576 | tf_op jit(solution)/shard_map/all_to_all | solution.py:216
Sparse Core Ops, SparseCore 0:
  10.5 82.8 all-gather.2

commit v8 on v7

--- a/solution.py
+++ b/solution.py
@@ -102,15 +102,14 @@
     idx_ref, w_ref, alpha_ref, packed_ref, out_ref,
     table, stage, spread, acc_ref, near, sems, near_sems,
 ):
-    buffers, batch, slots = near.shape
+    buffers, index_rows, _ = near.shape
     targets = w_ref.shape[0]
+    batch = targets // idx_ref.shape[0]
+    slots = index_rows * LANES // batch
     rounds = targets // (buffers * batch)
 
     def bring(r, b):
-        start = pl.multiple_of((r * buffers + b) * batch, batch)
-        return pltpu.make_async_copy(
-            idx_ref.at[pl.ds(start, batch), :], near.at[b], near_sems.at[b]
-        )
+        return pltpu.make_async_copy(idx_ref.at[r * buffers + b], near.at[b], near_sems.at[b])
 
     for b in range(buffers):
         bring(0, b).start()
@@ -131,7 +130,8 @@
                 for q in range(slots):
                     picked = None
                     for k in range(8):
-                        row = table[pl.ds(near[b, g + k, q], 1), :]
+                        at = (g + k) * slots + q
+                        row = table[pl.ds(near[b, at // LANES, at % LANES], 1), :]
                         row = jnp.broadcast_to(row, (8, LANES))
                         picked = row if k == 0 else jnp.where(lane_row == k, row, picked)
                     weight = jnp.take_along_axis(
@@ -157,6 +157,7 @@
 
 def sigma_block(pieces, idx, weights, alpha_term, packed, chunk=768, depth=4, buffers=4, batch=16):
     targets, slots = idx.shape
+    idx = idx.reshape(targets // batch, batch * slots // LANES, LANES)
     alphas = alpha_term.shape[0]
     _, classes, rows, _ = packed.shape
     pairs = classes * rows * Y
@@ -175,7 +176,7 @@
             pltpu.VMEM((depth, Y, chunk, LANES), jnp.bfloat16),
             pltpu.VMEM((Y // 2, 2 * LANES, 2 * LANES), jnp.bfloat16),
             pltpu.VMEM((targets, LANES), jnp.float32),
-            pltpu.SMEM((buffers, batch, slots), jnp.int32),
+            pltpu.SMEM((buffers, *idx.shape[1:]), jnp.int32),
             pltpu.SemaphoreType.DMA((depth,)),
             pltpu.SemaphoreType.DMA((buffers,)),
         ],

time: 186 us -> 185 us (level)
  no operation moved by 1% of the time
where the time goes in v8:
time: 185 us; the launch traced here: 184 us
  waiting for transfers between devices  44.3 us (24%)
  blocking collectives  43.6 us (24%)
  Pallas kernels  41.6 us (22%)
  starting transfers between devices  31.7 us (17%)
  between operations  13.5 us (7%)
  local copies, waits for them, and re-layouts  6.16 us (3%)
  other arithmetic  2.93 us (2%)
    all_to_all x1, blocking collectives, per_device(): lax.all_to_all(pieces, ('rep', 'row'), 0, 0, axis_index_groups=back, tile...  43.6 us
    pallas_call x1, Pallas kernels, sigma_block(): pl.pallas_call(functools.partial(sigma_kernel, chunk), in_specs=[pl.Block...  39.6 us
    all_to_all x1, waiting for transfers between devices, per_device(): lax.all_to_all(alpha_term, 'row', 0, 0, axis_index_groups=along_z)  23.3 us
    ppermute x1, starting transfers between devices, per_device(): got = lax.ppermute(sent, 'rep', [(0, 1), (1, 0)])  14.8 us
    all_to_all x1, waiting for transfers between devices, per_device(): columns = lax.all_to_all(pieces, 'row', 0, 0).reshape(strings, small)  13.8 us
    all_to_all x1, starting transfers between devices, per_device(): columns = lax.all_to_all(pieces, 'row', 0, 0).reshape(strings, small)  8.81 us
    all_to_all x1, starting transfers between devices, per_device(): lax.all_to_all(alpha_term, 'row', 0, 0, axis_index_groups=along_z)  8.1 us
    ppermute x1, waiting for transfers between devices, per_device(): got = lax.ppermute(sent, 'rep', [(0, 1), (1, 0)])  6.45 us
  transfers between devices with their start and end apart: 4, of which 4 were waited for; matrix products, arithmetic and copies ran while one was open for 5% of the time, Pallas kernels for 0%

profile of v8, /device:TPU:32, one launch (start us, length us, event | category | flops | bytes accessed | tf_op | source)
XLA Modules:
  0.0 184.2 jit_solution(1508575490834066409)
XLA Ops:
  6.5 0.0 copy-start
  6.5 0.0 all-gather.3.cloned.1.call-start
  6.5 2.0 %pack_rows.1 = bf16[1536,128]{1,0:T(8,128)(2,1)} custom-call(s32[1]{0:T(128)} %bitcast.8.turn_ref, bf16[16,12288]{1,0:T(8,128)(2,1)} %in_ref.1), custom_call_target="tpu_custom_call" | custom-call | tf_op jit(solution)/shard_map/pack_rows/pallas_call | solution.py:31
  8.5 0.0 all-gather.3.cloned.1.call-update
  8.6 1.0 constant_dynamic-slice_fusion.1
  9.5 1.0 constant_dynamic-slice_fusion.3
  10.5 14.8 %collective-permute-start = (f32[32,1536]{1,0:T(8,128)S(1)}, f32[32,1536]{1,0:T(8,128)S(1)}, u32[]{:S(2)}, u32[]{:S(2)}) collective-permute-start(f32[32,1536]{1,0:T(8,128)S(1)} %pad_maximum_fusion), channel_id=1, source_target_pairs={{0,1},{1,0},{2,3},{3,2},{4,5},{5,4},{6,7},{7,6},{8,9},{9,8},{10,11... | collective-permute-start | bytes 589832 | tf_op jit(solution)/shard_map/ppermute | solution.py:227
  25.4 0.9 constant_dynamic-slice_fusion
  26.3 0.3 reshape.25
  26.6 0.9 copy.42
  27.5 8.8 %all-to-all-start = ((bf16[32,16,192]{2,1,0:T(8,128)(2,1)}), bf16[32,16,192]{2,1,0:T(8,128)(2,1)S(1)}, u32[]{:S(2)}, u32[]{:S(2)}) async-start(bf16[32,16,192]{2,1,0:T(8,128)(2,1)} %copy.42), calls=%async_computation | async-start | bytes 524288 | tf_op jit(solution)/shard_map/all_to_all | solution.py:214
  36.3 6.5 %collective-permute-done = f32[32,1536]{1,0:T(8,128)S(1)} collective-permute-done((f32[32,1536]{1,0:T(8,128)S(1)}, f32[32,1536]{1,0:T(8,128)S(1)}, u32[]{:S(2)}, u32[]{:S(2)}) %collective-permute-start) | collective-permute-done | bytes 196640 | tf_op jit(solution)/shard_map/ppermute | solution.py:227
  42.8 0.3 copy.39
  43.1 13.8 %all-to-all-done = bf16[32,16,192]{2,1,0:T(8,128)(2,1)S(1)} async-done(((bf16[32,16,192]{2,1,0:T(8,128)(2,1)}), bf16[32,16,192]{2,1,0:T(8,128)(2,1)S(1)}, u32[]{:S(2)}, u32[]{:S(2)}) %all-to-all-start) | async-done | bytes 196640 | tf_op jit(solution)/shard_map/all_to_all | solution.py:214
  56.8 0.0 copy-done
  56.8 0.3 convolution_bitcast_fusion
  57.2 0.2 copy.43
  57.4 0.9 copy.44
  58.2 8.1 %all-to-all-start.1 = ((f32[8,4,16,192]{3,2,1,0:T(8,128)}), f32[8,4,16,192]{3,2,1,0:T(8,128)S(1)}, u32[]{:S(2)}, u32[]{:S(2)}) async-start(f32[8,4,16,192]{3,2,1,0:T(8,128)} %copy.44), calls=%async_computation.1 | async-start | bytes 1048576 | tf_op jit(solution)/shard_map/all_to_all | solution.py:217
  66.3 0.6 subtract_bitcast_fusion
  67.0 0.2 reshape.24.idx_ref
  67.2 0.3 copy.40
  67.5 0.6 broadcast_select_fusion.1
  68.1 0.7 maximum_bitcast_fusion.w_ref
  68.8 23.3 %all-to-all-done.1 = f32[8,4,16,192]{3,2,1,0:T(8,128)S(1)} async-done(((f32[8,4,16,192]{3,2,1,0:T(8,128)}), f32[8,4,16,192]{3,2,1,0:T(8,128)S(1)}, u32[]{:S(2)}, u32[]{:S(2)}) %all-to-all-start.1) | async-done | bytes 393248 | tf_op jit(solution)/shard_map/all_to_all | solution.py:217
  92.1 0.3 copy.45
  92.4 0.2 reshape.28.alpha_ref
  92.6 0.8 all-gather.3.cloned.1.call-done
  93.4 39.6 %sigma_block.1 = bf16[8,16,1536]{2,1,0:T(8,128)(2,1)S(1)} custom-call(s32[96,4,128]{2,1,0:T(4,128)S(1)} %reshape.24.idx_ref, f32[1536,128]{1,0:T(8,128)S(1)} %maximum_bitcast_fusion.w_ref, f32[64,1536]{1,0:T(8,128)S(1)} %reshape.28.alpha_ref, bf16[4,8,1536,128]{3,2,1,0:T(8,128)(2,1)} %bitcast.26), custom_call_target="tpu_custom_call" | custom-call | flops 6448742400 | bytes 13565952 | tf_op jit(solution)/shard_map/sigma_block/pallas_call | solution.py:164
  133.0 43.6 %all_to_all.15 = bf16[8,16,1536]{2,1,0:T(8,128)(2,1)S(1)} all-to-all(bf16[8,16,1536]{2,1,0:T(8,128)(2,1)S(1)} %sigma_block.1), channel_id=1, replica_groups={{0,128,256,384,1,129,257,385},{16,144,272,400,17,145,273,401},{32,160,2..., dimensions={0} | all-to-all | bytes 786432 | tf_op jit(solution)/shard_map/all_to_all | solution.py:247
  176.6 0.8 copy.47
  (4 shorter events, 0.1 us)
Async XLA Ops:
  6.5 50.3 %copy-start = (bf16[512,512]{1,0:T(8,128)(2,1)S(1)}, bf16[512,512]{1,0:T(8,128)(2,1)}, u32[]{:S(2)}) copy-start(bf16[512,512]{1,0:T(8,128)(2,1)} %param.5) | copy-start | bytes 1572868
  6.5 86.9 %all-gather.3.cloned.1.call-start = ((), (), s32[]{:S(2)}) async-start(), calls=%async_computation.3 | async-start | bytes 12976128 | tf_op jit(solution)/shard_map/all_gather | solution.py:208
  10.5 32.2 %collective-permute-start = (f32[32,1536]{1,0:T(8,128)S(1)}, f32[32,1536]{1,0:T(8,128)S(1)}, u32[]{:S(2)}, u32[]{:S(2)}) collective-permute-start(f32[32,1536]{1,0:T(8,128)S(1)} %pad_maximum_fusion), channel_id=1, source_target_pairs={{0,1},{1,0},{2,3},{3,2},{4,5},{5,4},{6,7},{7,6},{8,9},{9,8},{10,11... | collective-permute-start | bytes 589832 | tf_op jit(solution)/shard_map/ppermute | solution.py:227
  27.5 29.3 %all-to-all-start = ((bf16[32,16,192]{2,1,0:T(8,128)(2,1)}), bf16[32,16,192]{2,1,0:T(8,128)(2,1)S(1)}, u32[]{:S(2)}, u32[]{:S(2)}) async-start(bf16[32,16,192]{2,1,0:T(8,128)(2,1)} %copy.42), calls=%async_computation | async-start | bytes 524288 | tf_op jit(solution)/shard_map/all_to_all | solution.py:214
  58.2 33.9 %all-to-all-start.1 = ((f32[8,4,16,192]{3,2,1,0:T(8,128)}), f32[8,4,16,192]{3,2,1,0:T(8,128)S(1)}, u32[]{:S(2)}, u32[]{:S(2)}) async-start(f32[8,4,16,192]{3,2,1,0:T(8,128)} %copy.44), calls=%async_computation.1 | async-start | bytes 1048576 | tf_op jit(solution)/shard_map/all_to_all | solution.py:217
Sparse Core Ops, SparseCore 0:
  10.5 82.8 all-gather.2

commit v9 on v8

--- a/solution.py
+++ b/solution.py
@@ -242,10 +242,14 @@
     low, high = jnp.where(upper, 0.0, weights), jnp.where(upper, weights, 0.0)
     weights = jnp.concatenate([low, high] * (LANES // (2 * low.shape[0])), axis=0).T
 
-    pieces = sigma_block(reps * Y, idx, weights, alpha_term, packed)
-    back = [[r * Y * Z + y * Z + z for r in range(reps) for y in range(Y)] for z in range(Z)]
-    done = lax.all_to_all(pieces, ("rep", "row"), 0, 0, axis_index_groups=back, tiled=True)
-    return done.reshape(parts, own_rows, part).transpose(1, 0, 2).reshape(own_rows, betas)
+    pieces = sigma_block(Y, idx, weights, alpha_term, packed)
+    passed = lax.ppermute(pieces, "rep", [(0, 1), (1, 0)])
+    along_y = [[y * Z + z for y in range(Y)] for z in range(Z)]
+    here = lax.all_to_all(pieces, "row", 0, 0, axis_index_groups=along_y)
+    there = lax.all_to_all(passed, "row", 0, 0, axis_index_groups=along_y)
+    first, second = jnp.where(rep == 0, here, there), jnp.where(rep == 0, there, here)
+    done = jnp.concatenate([first, second], axis=0)
+    return done.transpose(1, 0, 2).reshape(own_rows, betas)
 
 
 def solution(mesh):

time: 185 us -> 180 us (0.973)
  the two profiles are of different devices: /device:TPU:32 before, /device:TPU:128 now
where the time goes in v9:
time: 180 us
  waiting for transfers between devices  60.4 us (34%)
  starting transfers between devices  44.5 us (25%)
  Pallas kernels  41.6 us (23%)
  between operations  13.6 us (8%)
  blocking collectives  10.1 us (6%)
  local copies, waits for them, and re-layouts  6.2 us (3%)
  other arithmetic  3 us (2%)
    pallas_call x1, Pallas kernels, sigma_block(): pl.pallas_call(functools.partial(sigma_kernel, chunk), in_specs=[pl.Block...  39.6 us
    all_to_all x1, waiting for transfers between devices, per_device(): lax.all_to_all(alpha_term, 'row', 0, 0, axis_index_groups=along_z)  19 us
    all_to_all x1, waiting for transfers between devices, per_device(): columns = lax.all_to_all(pieces, 'row', 0, 0).reshape(strings, small)  15.4 us
    ppermute x1, waiting for transfers between devices, per_device(): passed = lax.ppermute(pieces, 'rep', [(0, 1), (1, 0)])  11.6 us
    all_to_all x1, starting transfers between devices, per_device(): columns = lax.all_to_all(pieces, 'row', 0, 0).reshape(strings, small)  11.4 us
    ppermute x1, starting transfers between devices, per_device(): got = lax.ppermute(sent, 'rep', [(0, 1), (1, 0)])  10.9 us
    all_to_all x1, starting transfers between devices, per_device(): lax.all_to_all(alpha_term, 'row', 0, 0, axis_index_groups=along_z)  10.2 us
    all_to_all x1, blocking collectives, per_device(): here = lax.all_to_all(pieces, 'row', 0, 0, axis_index_groups=along_y)  10.1 us
  transfers between devices with their start and end apart: 6, of which 6 were waited for; matrix products, arithmetic and copies ran while one was open for 5% of the time, Pallas kernels for 0%

profile of v9, /device:TPU:128, one launch (start us, length us, event | category | flops | bytes accessed | tf_op | source)
XLA Modules:
  0.0 179.7 jit_solution(5948193590195055444)
XLA Ops:
  6.5 0.0 copy-start
  6.5 0.0 all-gather.3.cloned.1.call-start
  6.5 2.0 %pack_rows.1 = bf16[1536,128]{1,0:T(8,128)(2,1)} custom-call(s32[1]{0:T(128)} %bitcast.8.turn_ref, bf16[16,12288]{1,0:T(8,128)(2,1)} %in_ref.1), custom_call_target="tpu_custom_call" | custom-call | tf_op jit(solution)/shard_map/pack_rows/pallas_call | solution.py:31
  8.5 0.0 all-gather.3.cloned.1.call-update
  8.6 1.0 constant_dynamic-slice_fusion.1
  9.5 1.0 constant_dynamic-slice_fusion.3
  10.5 10.9 %collective-permute-start = (f32[32,1536]{1,0:T(8,128)S(1)}, f32[32,1536]{1,0:T(8,128)S(1)}, u32[]{:S(2)}, u32[]{:S(2)}) collective-permute-start(f32[32,1536]{1,0:T(8,128)S(1)} %pad_maximum_fusion), channel_id=1, source_target_pairs={{0,1},{1,0},{2,3},{3,2},{4,5},{5,4},{6,7},{7,6},{8,9},{9,8},{10,11... | collective-permute-start | bytes 589832 | tf_op jit(solution)/shard_map/ppermute | solution.py:227
  21.5 0.9 constant_dynamic-slice_fusion
  22.4 0.3 reshape.25
  22.7 0.9 copy.42
  23.6 11.4 %all-to-all-start = ((bf16[32,16,192]{2,1,0:T(8,128)(2,1)}), bf16[32,16,192]{2,1,0:T(8,128)(2,1)S(1)}, u32[]{:S(2)}, u32[]{:S(2)}) async-start(bf16[32,16,192]{2,1,0:T(8,128)(2,1)} %copy.42), calls=%async_computation | async-start | bytes 524288 | tf_op jit(solution)/shard_map/all_to_all | solution.py:214
  35.0 2.7 %collective-permute-done = f32[32,1536]{1,0:T(8,128)S(1)} collective-permute-done((f32[32,1536]{1,0:T(8,128)S(1)}, f32[32,1536]{1,0:T(8,128)S(1)}, u32[]{:S(2)}, u32[]{:S(2)}) %collective-permute-start) | collective-permute-done | bytes 196640 | tf_op jit(solution)/shard_map/ppermute | solution.py:227
  37.7 0.3 copy.39
  38.0 15.4 %all-to-all-done = bf16[32,16,192]{2,1,0:T(8,128)(2,1)S(1)} async-done(((bf16[32,16,192]{2,1,0:T(8,128)(2,1)}), bf16[32,16,192]{2,1,0:T(8,128)(2,1)S(1)}, u32[]{:S(2)}, u32[]{:S(2)}) %all-to-all-start) | async-done | bytes 196640 | tf_op jit(solution)/shard_map/all_to_all | solution.py:214
  53.4 0.0 copy-done
  53.4 0.3 convolution_bitcast_fusion
  53.7 0.2 copy.43
  54.0 0.9 copy.44
  54.8 10.2 %all-to-all-start.1 = ((f32[8,4,16,192]{3,2,1,0:T(8,128)}), f32[8,4,16,192]{3,2,1,0:T(8,128)S(1)}, u32[]{:S(2)}, u32[]{:S(2)}) async-start(f32[8,4,16,192]{3,2,1,0:T(8,128)} %copy.44), calls=%async_computation.1 | async-start | bytes 1048576 | tf_op jit(solution)/shard_map/all_to_all | solution.py:217
  65.0 0.6 subtract_bitcast_fusion
  65.6 0.2 reshape.24.idx_ref
  65.9 0.3 copy.40
  66.2 0.6 broadcast_select_fusion.1
  66.8 0.7 maximum_bitcast_fusion.w_ref
  67.5 19.0 %all-to-all-done.1 = f32[8,4,16,192]{3,2,1,0:T(8,128)S(1)} async-done(((f32[8,4,16,192]{3,2,1,0:T(8,128)}), f32[8,4,16,192]{3,2,1,0:T(8,128)S(1)}, u32[]{:S(2)}, u32[]{:S(2)}) %all-to-all-start.1) | async-done | bytes 393248 | tf_op jit(solution)/shard_map/all_to_all | solution.py:217
  86.4 0.3 copy.45
  86.7 0.2 reshape.28.alpha_ref
  86.9 5.4 %all-gather.3.cloned.1.call-done = bf16[49152,128]{1,0:T(8,128)(2,1)} async-done(((bf16[1536,128]{1,0:T(8,128)(2,1)}), bf16[49152,128]{1,0:T(8,128)(2,1)}) %all-gather.3.cloned.1.call-update) | async-done | bytes 12582928 | tf_op jit(solution)/shard_map/all_gather | solution.py:208
  92.3 39.6 %sigma_block.1 = bf16[4,16,1536]{2,1,0:T(8,128)(2,1)S(1)} custom-call(s32[96,4,128]{2,1,0:T(4,128)S(1)} %reshape.24.idx_ref, f32[1536,128]{1,0:T(8,128)S(1)} %maximum_bitcast_fusion.w_ref, f32[64,1536]{1,0:T(8,128)S(1)} %reshape.28.alpha_ref, bf16[4,8,1536,128]{3,2,1,0:T(8,128)(2,1)} %bitcast.26), custom_call_target="tpu_custom_call" | custom-call | flops 6448742400 | bytes 13565952 | tf_op jit(solution)/shard_map/sigma_block/pallas_call | solution.py:164
  131.9 8.0 %collective-permute-start.1 = (bf16[4,16,1536]{2,1,0:T(8,128)(2,1)S(1)}, bf16[4,16,1536]{2,1,0:T(8,128)(2,1)}, u32[]{:S(2)}, u32[]{:S(2)}) collective-permute-start(bf16[4,16,1536]{2,1,0:T(8,128)(2,1)S(1)} %sigma_block.1), channel_id=1, source_target_pairs={{0,1},{1,0},{2,3},{3,2},{4,5},{5,4},{6,7},{7,6},{8,9},{9,8},{10,11... | collective-permute-start | bytes 589832 | tf_op jit(solution)/shard_map/ppermute | solution.py:246
  139.9 10.1 %all_to_all.20 = bf16[4,16,1536]{2,1,0:T(8,128)(2,1)S(1)} all-to-all(bf16[4,16,1536]{2,1,0:T(8,128)(2,1)S(1)} %sigma_block.1), channel_id=1, replica_groups={{0,128,256,384},{16,144,272,400},{32,160,288,416},{48,176,304,432},{64,..., dimensions={0} | all-to-all | bytes 393216 | tf_op jit(solution)/shard_map/all_to_all | solution.py:248
  150.0 11.6 %collective-permute-done.1 = bf16[4,16,1536]{2,1,0:T(8,128)(2,1)} collective-permute-done((bf16[4,16,1536]{2,1,0:T(8,128)(2,1)S(1)}, bf16[4,16,1536]{2,1,0:T(8,128)(2,1)}, u32[]{:S(2)}, u32[]{:S(2)}) %collective-permute-start.1) | collective-permute-done | bytes 196640 | tf_op jit(solution)/shard_map/ppermute | solution.py:246
  161.6 4.1 %all-to-all-start.3 = ((bf16[4,16,1536]{2,1,0:T(8,128)(2,1)}), bf16[4,16,1536]{2,1,0:T(8,128)(2,1)S(1)}, u32[]{:S(2)}, u32[]{:S(2)}) async-start(bf16[4,16,1536]{2,1,0:T(8,128)(2,1)} %collective-permute-done.1), calls=%async_computation.3 | async-start | bytes 393216 | tf_op jit(solution)/shard_map/all_to_all | solution.py:249
  165.7 6.3 %all-to-all-done.3 = bf16[4,16,1536]{2,1,0:T(8,128)(2,1)S(1)} async-done(((bf16[4,16,1536]{2,1,0:T(8,128)(2,1)}), bf16[4,16,1536]{2,1,0:T(8,128)(2,1)S(1)}, u32[]{:S(2)}, u32[]{:S(2)}) %all-to-all-start.3) | async-done | bytes 196640 | tf_op jit(solution)/shard_map/all_to_all | solution.py:249
  172.1 0.8 copy.47
  (6 shorter events, 0.1 us)
Async XLA Ops:
  6.5 46.9 %copy-start = (bf16[512,512]{1,0:T(8,128)(2,1)S(1)}, bf16[512,512]{1,0:T(8,128)(2,1)}, u32[]{:S(2)}) copy-start(bf16[512,512]{1,0:T(8,128)(2,1)} %param.5) | copy-start | bytes 1572868
  6.5 85.8 %all-gather.3.cloned.1.call-start = ((), (), s32[]{:S(2)}) async-start(), calls=%async_computation.4 | async-start | bytes 12976128 | tf_op jit(solution)/shard_map/all_gather | solution.py:208
  10.5 27.1 %collective-permute-start = (f32[32,1536]{1,0:T(8,128)S(1)}, f32[32,1536]{1,0:T(8,128)S(1)}, u32[]{:S(2)}, u32[]{:S(2)}) collective-permute-start(f32[32,1536]{1,0:T(8,128)S(1)} %pad_maximum_fusion), channel_id=1, source_target_pairs={{0,1},{1,0},{2,3},{3,2},{4,5},{5,4},{6,7},{7,6},{8,9},{9,8},{10,11... | collective-permute-start | bytes 589832 | tf_op jit(solution)/shard_map/ppermute | solution.py:227
  23.6 29.8 %all-to-all-start = ((bf16[32,16,192]{2,1,0:T(8,128)(2,1)}), bf16[32,16,192]{2,1,0:T(8,128)(2,1)S(1)}, u32[]{:S(2)}, u32[]{:S(2)}) async-start(bf16[32,16,192]{2,1,0:T(8,128)(2,1)} %copy.42), calls=%async_computation | async-start | bytes 524288 | tf_op jit(solution)/shard_map/all_to_all | solution.py:214
  54.8 31.6 %all-to-all-start.1 = ((f32[8,4,16,192]{3,2,1,0:T(8,128)}), f32[8,4,16,192]{3,2,1,0:T(8,128)S(1)}, u32[]{:S(2)}, u32[]{:S(2)}) async-start(f32[8,4,16,192]{3,2,1,0:T(8,128)} %copy.44), calls=%async_computation.1 | async-start | bytes 1048576 | tf_op jit(solution)/shard_map/all_to_all | solution.py:217
  131.9 29.7 %collective-permute-start.1 = (bf16[4,16,1536]{2,1,0:T(8,128)(2,1)S(1)}, bf16[4,16,1536]{2,1,0:T(8,128)(2,1)}, u32[]{:S(2)}, u32[]{:S(2)}) collective-permute-start(bf16[4,16,1536]{2,1,0:T(8,128)(2,1)S(1)} %sigma_block.1), channel_id=1, source_target_pairs={{0,1},{1,0},{2,3},{3,2},{4,5},{5,4},{6,7},{7,6},{8,9},{9,8},{10,11... | collective-permute-start | bytes 589832 | tf_op jit(solution)/shard_map/ppermute | solution.py:246
  161.6 10.4 %all-to-all-start.3 = ((bf16[4,16,1536]{2,1,0:T(8,128)(2,1)}), bf16[4,16,1536]{2,1,0:T(8,128)(2,1)S(1)}, u32[]{:S(2)}, u32[]{:S(2)}) async-start(bf16[4,16,1536]{2,1,0:T(8,128)(2,1)} %collective-permute-done.1), calls=%async_computation.3 | async-start | bytes 393216 | tf_op jit(solution)/shard_map/all_to_all | solution.py:249
Sparse Core Ops, SparseCore 0:
  10.5 81.7 all-gather.2
